TPU v7x, 128 devices: a whole 4x4x4 slice. The times are simulated.
128 devices in a mesh: ctx: 16 (over y, z), exp: 8 (over x, core).
Axes of the slice: x: 4, y: 4, z: 4, core: 2. Of those that a mesh axis runs over, the one named last changes fastest.
Arguments:
- span_q: bfloat16 [1024, 5120], P('ctx', 'exp'), may hold values from -12 to 12
- decode_q: bfloat16 [1024, 5120], P('ctx', 'exp'), may hold values from -12 to 12
- k_cache: bfloat16 [49152, 1024], P('ctx', 'exp'), may hold values from -12 to 12
- v_cache: bfloat16 [49152, 1024], P('ctx', 'exp'), may hold values from -6 to 6
- span_k: bfloat16 [1024, 1024], P('ctx', 'exp'), may hold values from -6 to 6
- span_v: bfloat16 [1024, 1024], P('ctx', 'exp'), may hold values from -6 to 6
- decode_k: bfloat16 [1024, 1024], P('ctx', 'exp'), may hold values from -6 to 6
- decode_v: bfloat16 [1024, 1024], P('ctx', 'exp'), may hold values from -6 to 6
- decode_pos: int32 [1024], replicated, may hold values from 2 to 49152
- out_weight: bfloat16 [5120, 5120], P('exp'), may hold values from -0.078125 to 0.078125
- span_resid: bfloat16 [1024, 5120], P(('ctx', 'exp')), may hold values from -3 to 3
- decode_resid: bfloat16 [1024, 5120], P(('ctx', 'exp')), may hold values from -3 to 3
- norm_gain: bfloat16 [5120], replicated, may hold values from 0.099609375 to 1.8984375
- router: bfloat16 [5120, 8], replicated, may hold values from -0.15625 to 0.15625
- span_expert: int32 [1024, 1], P(('ctx', 'exp')), may hold values from 0 to 7; in each aligned block of 8 rows (0 to 7, 8 to 15, ...) at most 2 rows name the same one
- decode_expert: int32 [1024, 1], P(('ctx', 'exp')), may hold values from 0 to 7; in each aligned block of 8 rows (0 to 7, 8 to 15, ...) at most 2 rows name the same one
- w_gate: bfloat16 [8, 5120, 8192], P('exp', None, 'ctx'), may hold values from -0.078125 to 0.078125
- w_up: bfloat16 [8, 5120, 8192], P('exp', None, 'ctx'), may hold values from -0.078125 to 0.078125
- w_down: bfloat16 [8, 8192, 5120], P('exp', 'ctx'), may hold values from -0.0625 to 0.0625
Outputs:
- span_out: bfloat16 [1024, 5120], P(('ctx', 'exp'))
- decode_out: bfloat16 [1024, 5120], P(('ctx', 'exp'))
Inputs may be any that keep to these rules, and one draw needn't show every extreme that they name: `span_expert`: among the rows of one device, no expert is chosen by more than 2 rows. `decode_expert`: among the rows of one device, no expert is chosen by more than 2 rows.
All inputs are finite; a program needn't handle non-finite values.
Results may differ from a plain program's by a relative error of at most 0.015.
Values may be sent and summed in bfloat16 or wider, within the bound.
A program may use at most 192 MiB of HBM per device.

v0:
```python
import math

import jax
import jax.numpy as jnp
from jax import lax
from jax.sharding import PartitionSpec as P

HEADS = 40
KV_HEADS = 8
HEAD = 128


NEG = -1e30
EPS = 1e-05


def on_device(
    span_q,
    decode_q,
    k_cache,
    v_cache,
    span_k,
    span_v,
    decode_k,
    decode_v,
    decode_pos,
    out_weight,
    span_resid,
    decode_resid,
    norm_gain,
    router,
    span_expert,
    decode_expert,
    w_gate,
    w_up,
    w_down,
):
    tok_rows = span_q.shape[0]
    row_width = span_q.shape[1]
    pre_rows = k_cache.shape[0]
    kv_heads_here = k_cache.shape[1] // HEAD
    head_group = HEADS // KV_HEADS
    heads_local = kv_heads_here * head_group
    model_width = span_resid.shape[1]
    exp_count = lax.axis_size("exp")
    score_scale = HEAD ** (-0.5)
    ctx_index = lax.axis_index("ctx")
    key_pre = k_cache.reshape(pre_rows, kv_heads_here, HEAD)
    val_pre = v_cache.reshape(pre_rows, kv_heads_here, HEAD)
    key_span = span_k.reshape(tok_rows, kv_heads_here, HEAD)
    val_span = span_v.reshape(tok_rows, kv_heads_here, HEAD)
    prefix_pos = ctx_index * pre_rows + jnp.arange(pre_rows, dtype=jnp.int32)
    span_pos = ctx_index * tok_rows + jnp.arange(tok_rows, dtype=jnp.int32)

    def attend_block(queries, first_row):
        block_rows = queries.shape[0]
        row_ids = first_row + jnp.arange(block_rows, dtype=jnp.int32)
        limits = lax.dynamic_slice_in_dim(decode_pos, first_row, block_rows, 0)
        score_pre = (
            jnp.einsum("bskgd,jkd->bskgj", queries, key_pre, preferred_element_type=jnp.float32)
            * score_scale
        )
        score_span = (
            jnp.einsum("bskgd,jkd->bskgj", queries, key_span, preferred_element_type=jnp.float32)
            * score_scale
        )
        seen_pre = jnp.stack(
            [jnp.ones((block_rows, pre_rows), bool), prefix_pos[None, :] < limits[:, None]], 1
        )[:, :, None, None, :]
        seen_span = jnp.stack(
            [span_pos[None, :] <= row_ids[:, None], jnp.zeros((block_rows, tok_rows), bool)], 1
        )[:, :, None, None, :]
        score_pre = jnp.where(seen_pre, score_pre, NEG)
        score_span = jnp.where(seen_span, score_span, NEG)
        top_max = jnp.maximum(jnp.max(score_pre, -1), jnp.max(score_span, -1))
        weight_pre = jnp.where(seen_pre, jnp.exp(score_pre - top_max[..., None]), 0.0)
        weight_span = jnp.where(seen_span, jnp.exp(score_span - top_max[..., None]), 0.0)
        denom_part = jnp.sum(weight_pre, -1) + jnp.sum(weight_span, -1)
        numer_part = jnp.einsum(
            "bskgj,jkd->bskgd",
            weight_pre.astype(jnp.bfloat16),
            val_pre,
            preferred_element_type=jnp.float32,
        )
        numer_part = numer_part + jnp.einsum(
            "bskgj,jkd->bskgd",
            weight_span.astype(jnp.bfloat16),
            val_span,
            preferred_element_type=jnp.float32,
        )
        return (
            numer_part.reshape(block_rows, 2, row_width),
            denom_part.reshape(block_rows, 2, heads_local),
            top_max.reshape(block_rows, 2, heads_local),
        )

    queries = jnp.stack([span_q, decode_q], 1)
    shard_rows = lax.all_gather(queries, "ctx", axis=0, tiled=True)
    row_count = shard_rows.shape[0]
    block_rows = math.gcd(row_count, 256)
    step_count = row_count // block_rows
    shaped = shard_rows.reshape(step_count, block_rows, 2, kv_heads_here, head_group, HEAD)
    firsts = block_rows * jnp.arange(step_count, dtype=jnp.int32)

    def one_block(packed):
        return attend_block(packed[0], packed[1])

    numer_part, denom_part, top_max = lax.map(one_block, (shaped, firsts))
    numer_part, denom_part, top_max = (
        numer_part.reshape(row_count, 2, row_width),
        denom_part.reshape(row_count, 2, heads_local),
        top_max.reshape(row_count, 2, heads_local),
    )
    top_every = lax.pmax(top_max, "ctx")
    factor = jnp.exp(top_max - top_every)
    scaled_numer = (numer_part.reshape(-1, 2, heads_local, HEAD) * factor[..., None]).reshape(
        -1, 2, row_width
    )
    numer_sum, denom_sum = (
        lax.psum_scatter(scaled_numer, "ctx", scatter_dimension=0, tiled=True),
        lax.psum_scatter(denom_part * factor, "ctx", scatter_dimension=0, tiled=True),
    )
    numer_sum = numer_sum.reshape(tok_rows, 2, heads_local, HEAD)
    top_all = lax.dynamic_slice_in_dim(top_every, ctx_index * tok_rows, tok_rows, 0)
    dec_query = decode_q.reshape(tok_rows, kv_heads_here, head_group, HEAD).astype(jnp.float32)
    dec_key = decode_k.reshape(tok_rows, kv_heads_here, HEAD).astype(jnp.float32)
    own_score = (jnp.sum(dec_query * dec_key[:, :, None, :], -1) * score_scale).reshape(
        tok_rows, heads_local
    )
    own_score = jnp.stack([jnp.full_like(own_score, NEG), own_score], 1)
    dec_val = decode_v.reshape(tok_rows, kv_heads_here, HEAD).astype(jnp.float32)
    own_val = jnp.stack([jnp.zeros_like(dec_val), dec_val], 1)
    total_max = jnp.maximum(top_all, own_score)
    scale_top = jnp.exp(top_all - total_max).reshape(tok_rows, 2, kv_heads_here, head_group)
    own_weight = jnp.exp(own_score - total_max).reshape(tok_rows, 2, kv_heads_here, head_group)
    numer = (
        numer_sum.reshape(tok_rows, 2, kv_heads_here, head_group, HEAD) * scale_top[..., None]
        + own_weight[..., None] * own_val[:, :, :, None, :]
    )
    denom = denom_sum.reshape(tok_rows, 2, kv_heads_here, head_group) * scale_top + own_weight
    attn = (numer / denom[..., None]).astype(jnp.bfloat16).reshape(tok_rows, 2, row_width)
    projected = lax.psum_scatter(
        jnp.einsum("rsw,wd->rsd", attn, out_weight, preferred_element_type=jnp.float32),
        "exp",
        scatter_dimension=0,
        tiled=True,
    )
    stream = projected + jnp.stack([span_resid, decode_resid], 1).astype(jnp.float32)
    normed = (
        stream
        * lax.rsqrt(jnp.mean(stream * stream, -1, keepdims=True) + EPS)
        * norm_gain.astype(jnp.float32)
    ).astype(jnp.bfloat16)
    expert_ids = jnp.stack([span_expert[:, 0], decode_expert[:, 0]], 1)
    rows_here = expert_ids.shape[0]
    expert_total = router.shape[1]
    logits = jnp.einsum("rsd,de->rse", normed, router, preferred_element_type=jnp.float32)
    expert_iota = jnp.arange(expert_total, dtype=jnp.int32)
    picked_logit = jnp.sum(jnp.where(expert_ids[..., None] == expert_iota, logits, 0.0), -1)
    gate_value = jax.nn.sigmoid(picked_logit)
    routed_in = (normed.astype(jnp.float32) * gate_value[..., None]).astype(jnp.bfloat16)
    capacity = 2 * tok_rows // (exp_count * exp_count)
    row_order = jnp.arange(rows_here, dtype=jnp.int32)
    same_expert = expert_ids[:, None, :] == expert_ids[None, :, :]
    slot_index = jnp.sum(same_expert & (row_order[None, :] < row_order[:, None])[:, :, None], 1)
    column = (
        expert_ids * (2 * capacity)
        + jnp.arange(2, dtype=jnp.int32)[None, :] * capacity
        + slot_index
    ).reshape(-1)
    slot_total = expert_total * 2 * capacity
    onehot = (column[:, None] == jnp.arange(slot_total, dtype=jnp.int32)[None, :]).astype(
        jnp.bfloat16
    )
    flat_rows = routed_in.reshape(rows_here * 2, model_width)
    buffer = jnp.einsum("rc,rd->cd", onehot, flat_rows, preferred_element_type=jnp.float32).astype(
        jnp.bfloat16
    )
    arrived = lax.all_to_all(buffer, "exp", split_axis=0, concat_axis=0, tiled=True)
    shard_rows = lax.all_gather(arrived, "ctx", axis=0, tiled=True)
    gate_h = jnp.dot(shard_rows, w_gate[0], preferred_element_type=jnp.float32)
    up_h = jnp.dot(shard_rows, w_up[0], preferred_element_type=jnp.float32)
    hidden = (jax.nn.silu(gate_h) * up_h).astype(jnp.bfloat16)
    partial_out = jnp.dot(hidden, w_down[0], preferred_element_type=jnp.float32).astype(
        jnp.bfloat16
    )
    summed = lax.psum_scatter(
        partial_out.astype(jnp.float32).astype(jnp.bfloat16), "ctx", scatter_dimension=0, tiled=True
    )
    returned = lax.all_to_all(summed, "exp", split_axis=0, concat_axis=0, tiled=True)
    routed = jnp.einsum("rc,cd->rd", onehot, returned, preferred_element_type=jnp.float32).reshape(
        rows_here, 2, model_width
    )
    result = (stream + routed).astype(jnp.bfloat16)
    return (result[:, 0], result[:, 1])


def solution(mesh):
    in_specs = (
        P("ctx", "exp"),
        P("ctx", "exp"),
        P("ctx", "exp"),
        P("ctx", "exp"),
        P("ctx", "exp"),
        P("ctx", "exp"),
        P("ctx", "exp"),
        P("ctx", "exp"),
        P(),
        P("exp", None),
        P(("ctx", "exp"), None),
        P(("ctx", "exp"), None),
        P(),
        P(),
        P(("ctx", "exp"), None),
        P(("ctx", "exp"), None),
        P("exp", None, "ctx"),
        P("exp", None, "ctx"),
        P("exp", "ctx", None),
    )
    out_specs = (P(("ctx", "exp"), None), P(("ctx", "exp"), None))
    return jax.shard_map(
        on_device, mesh=mesh, in_specs=in_specs, out_specs=out_specs, check_vma=False
    )
```

profile of v0, /device:TPU:1, one launch (start us, length us, event | category | flops | bytes accessed | tf_op | source)
XLA Modules:
  0.0 738.0 jit_solution(14059922380492334482)
XLA Ops:
  11.2 48.3 %all-gather.3.cloned.1.call-done = bf16[1024,2,640]{2,0,1:T(8,128)(2,1)} async-done(((bf16[64,2,640]{2,0,1:T(8,128)(2,1)}), bf16[1024,2,640]{2,0,1:T(8,128)(2,1)}) %all-gather.3.cloned.1.call-update) | async-done | bytes 2621456 | tf_op jit(solution)/shard_map/all_gather | solution.py:98
  59.5 7.0 reshape.387
  70.9 207.5 %while.15 = (s32[]{:T(128)}, f32[4,256,2,640]{3,1,0,2:T(8,128)}, f32[4,256,2,5]{1,0,2,3:T(4,128)S(1)}, f32[4,256,2,5]{1,0,2,3:T(4,128)S(1)}, s32[4]{0:T(128)S(1)...) while((s32[]{:T(128)}, f32[4,256,2,640]{3,1,0,2:T(8,128)}, ...), condition=%wide.region_5.6_spmd.clone, body=%wide.region_0.5_spmd.clone.sunk | while | flops 4215257344 | bytes 116714728 | solution.py:108
  74.9 14.4 %fusion.85 = (f32[256,2,5]{0,2,1:T(8,128)S(1)}, f32[256,2,5,3072]{3,0,2,1:T(8,128)}) fusion(pred[256,2,3072]{2,0,1:T(8,128)(4,1)S(1)} %stack.63, bf16[3072,1,128]{2,0,1:T(8,128)(2,1)} %get-tuple-element.337, bf16[4,256,2,1,5,128]{5,1,4,2,3,0:T(8,128)(2,1)} %get-tuple-element.336, s32[]{:T(128)} %get-tuple-element.312), kind=kOutput, calls=%fused_computation.4.clone.1 | convolution fusion | flops 2036856320 | bytes 34482688 | tf_op jit(solution)/shard_map/while/body/eval_jaxpr/bskgd,jkd->bskgj/dot_general | solution.py:60
  91.6 15.1 %fusion.88 = f32[256,2,5]{0,2,1:T(8,128)S(1)} fusion(f32[256,2,5,3072]{3,0,2,1:T(8,128)} %get-tuple-element.293, f32[256,2,5]{0,2,1:T(8,128)S(1)} %max.36, pred[256,2,3072]{2,0,1:T(8,128)(4,1)S(1)} %stack.63), kind=kLoop, calls=%fused_computation.5.clone.1 | loop fusion | flops 39319040 | bytes 33050624 | tf_op jit(solution)/shard_map/while/body/eval_jaxpr/reduce_sum | solution.py:78
  107.3 13.8 %fusion.87 = f32[256,2,5,128]{0,3,2,1:T(8,128)S(1)} fusion(f32[256,2,5,128]{0,3,2,1:T(8,128)S(1)} %fusion.86, f32[256,2,5,3072]{3,0,2,1:T(8,128)} %get-tuple-element.293, f32[256,2,5]{0,2,1:T(8,128)S(1)} %max.36, pred[256,2,3072]{2,0,1:T(8,128)(4,1)S(1)} %stack.63, bf16[3072,1,128]{0,2,1:T(8,128)(2,1)} %get-tuple-element.339), kind=kOutput, calls=%fused_computation.11.clone.1 | convolution fusion | flops 2052915200 | bytes 36448256 | tf_op jit(solution)/shard_map/while/body/eval_jaxpr/bskgj,jkd->bskgd/dot_general | solution.py:79
  126.8 14.4 %fusion.85 = (f32[256,2,5]{0,2,1:T(8,128)S(1)}, f32[256,2,5,3072]{3,0,2,1:T(8,128)}) fusion(pred[256,2,3072]{2,0,1:T(8,128)(4,1)S(1)} %stack.63, bf16[3072,1,128]{2,0,1:T(8,128)(2,1)} %get-tuple-element.337, bf16[4,256,2,1,5,128]{5,1,4,2,3,0:T(8,128)(2,1)} %get-tuple-element.336, s32[]{:T(128)} %get-tuple-element.312), kind=kOutput, calls=%fused_computation.4.clone.1 | convolution fusion | flops 2036856320 | bytes 34482688 | tf_op jit(solution)/shard_map/while/body/eval_jaxpr/bskgd,jkd->bskgj/dot_general | solution.py:60
  143.4 15.1 %fusion.88 = f32[256,2,5]{0,2,1:T(8,128)S(1)} fusion(f32[256,2,5,3072]{3,0,2,1:T(8,128)} %get-tuple-element.293, f32[256,2,5]{0,2,1:T(8,128)S(1)} %max.36, pred[256,2,3072]{2,0,1:T(8,128)(4,1)S(1)} %stack.63), kind=kLoop, calls=%fused_computation.5.clone.1 | loop fusion | flops 39319040 | bytes 33050624 | tf_op jit(solution)/shard_map/while/body/eval_jaxpr/reduce_sum | solution.py:78
  159.2 13.8 %fusion.87 = f32[256,2,5,128]{0,3,2,1:T(8,128)S(1)} fusion(f32[256,2,5,128]{0,3,2,1:T(8,128)S(1)} %fusion.86, f32[256,2,5,3072]{3,0,2,1:T(8,128)} %get-tuple-element.293, f32[256,2,5]{0,2,1:T(8,128)S(1)} %max.36, pred[256,2,3072]{2,0,1:T(8,128)(4,1)S(1)} %stack.63, bf16[3072,1,128]{0,2,1:T(8,128)(2,1)} %get-tuple-element.339), kind=kOutput, calls=%fused_computation.11.clone.1 | convolution fusion | flops 2052915200 | bytes 36448256 | tf_op jit(solution)/shard_map/while/body/eval_jaxpr/bskgj,jkd->bskgd/dot_general | solution.py:79
  178.7 14.4 %fusion.85 = (f32[256,2,5]{0,2,1:T(8,128)S(1)}, f32[256,2,5,3072]{3,0,2,1:T(8,128)}) fusion(pred[256,2,3072]{2,0,1:T(8,128)(4,1)S(1)} %stack.63, bf16[3072,1,128]{2,0,1:T(8,128)(2,1)} %get-tuple-element.337, bf16[4,256,2,1,5,128]{5,1,4,2,3,0:T(8,128)(2,1)} %get-tuple-element.336, s32[]{:T(128)} %get-tuple-element.312), kind=kOutput, calls=%fused_computation.4.clone.1 | convolution fusion | flops 2036856320 | bytes 34482688 | tf_op jit(solution)/shard_map/while/body/eval_jaxpr/bskgd,jkd->bskgj/dot_general | solution.py:60
  195.3 15.1 %fusion.88 = f32[256,2,5]{0,2,1:T(8,128)S(1)} fusion(f32[256,2,5,3072]{3,0,2,1:T(8,128)} %get-tuple-element.293, f32[256,2,5]{0,2,1:T(8,128)S(1)} %max.36, pred[256,2,3072]{2,0,1:T(8,128)(4,1)S(1)} %stack.63), kind=kLoop, calls=%fused_computation.5.clone.1 | loop fusion | flops 39319040 | bytes 33050624 | tf_op jit(solution)/shard_map/while/body/eval_jaxpr/reduce_sum | solution.py:78
  211.1 13.8 %fusion.87 = f32[256,2,5,128]{0,3,2,1:T(8,128)S(1)} fusion(f32[256,2,5,128]{0,3,2,1:T(8,128)S(1)} %fusion.86, f32[256,2,5,3072]{3,0,2,1:T(8,128)} %get-tuple-element.293, f32[256,2,5]{0,2,1:T(8,128)S(1)} %max.36, pred[256,2,3072]{2,0,1:T(8,128)(4,1)S(1)} %stack.63, bf16[3072,1,128]{0,2,1:T(8,128)(2,1)} %get-tuple-element.339), kind=kOutput, calls=%fused_computation.11.clone.1 | convolution fusion | flops 2052915200 | bytes 36448256 | tf_op jit(solution)/shard_map/while/body/eval_jaxpr/bskgj,jkd->bskgd/dot_general | solution.py:79
  230.6 14.4 %fusion.85 = (f32[256,2,5]{0,2,1:T(8,128)S(1)}, f32[256,2,5,3072]{3,0,2,1:T(8,128)}) fusion(pred[256,2,3072]{2,0,1:T(8,128)(4,1)S(1)} %stack.63, bf16[3072,1,128]{2,0,1:T(8,128)(2,1)} %get-tuple-element.337, bf16[4,256,2,1,5,128]{5,1,4,2,3,0:T(8,128)(2,1)} %get-tuple-element.336, s32[]{:T(128)} %get-tuple-element.312), kind=kOutput, calls=%fused_computation.4.clone.1 | convolution fusion | flops 2036856320 | bytes 34482688 | tf_op jit(solution)/shard_map/while/body/eval_jaxpr/bskgd,jkd->bskgj/dot_general | solution.py:60
  247.2 15.1 %fusion.88 = f32[256,2,5]{0,2,1:T(8,128)S(1)} fusion(f32[256,2,5,3072]{3,0,2,1:T(8,128)} %get-tuple-element.293, f32[256,2,5]{0,2,1:T(8,128)S(1)} %max.36, pred[256,2,3072]{2,0,1:T(8,128)(4,1)S(1)} %stack.63), kind=kLoop, calls=%fused_computation.5.clone.1 | loop fusion | flops 39319040 | bytes 33050624 | tf_op jit(solution)/shard_map/while/body/eval_jaxpr/reduce_sum | solution.py:78
  263.0 13.8 %fusion.87 = f32[256,2,5,128]{0,3,2,1:T(8,128)S(1)} fusion(f32[256,2,5,128]{0,3,2,1:T(8,128)S(1)} %fusion.86, f32[256,2,5,3072]{3,0,2,1:T(8,128)} %get-tuple-element.293, f32[256,2,5]{0,2,1:T(8,128)S(1)} %max.36, pred[256,2,3072]{2,0,1:T(8,128)(4,1)S(1)} %stack.63, bf16[3072,1,128]{0,2,1:T(8,128)(2,1)} %get-tuple-element.339), kind=kOutput, calls=%fused_computation.11.clone.1 | convolution fusion | flops 2052915200 | bytes 36448256 | tf_op jit(solution)/shard_map/while/body/eval_jaxpr/bskgj,jkd->bskgd/dot_general | solution.py:79
  278.5 58.2 %pmax.7 = f32[1024,2,5]{0,1,2:T(2,128)S(1)} all-reduce(f32[1024,2,5]{0,1,2:T(2,128)S(1)} %reshape.368), channel_id=1, replica_groups=mesh['ctx'=16,'exp'=8] {'ctx'}, use_global_device_ids=true, to_apply=%region_6.7 | all-reduce | flops 10240 | bytes 81920 | tf_op jit(solution)/shard_map/pmax | solution.py:114
  360.5 64.2 %reduce-scatter.13.cloned.1.call-done = f32[64,10]{1,0:T(8,128)} async-done(((f32[1024,10]{1,0:T(8,128)}), f32[64,10]{1,0:T(8,128)}) %reduce-scatter.13.cloned.1.call-update) | async-done | bytes 2576
  427.1 80.5 %reduce-scatter.7.cloned.1.call-done = f32[64,2,640]{2,0,1:T(8,128)} async-done(((f32[1024,2,640]{2,0,1:T(8,128)}), f32[64,2,640]{2,0,1:T(8,128)}) %reduce-scatter.7.cloned.1.call-update) | async-done | bytes 327696 | tf_op jit(solution)/shard_map/reduce_scatter | solution.py:120
  513.9 31.7 %reduce-scatter.9.cloned.1.call-done = f32[8,2,5120]{2,0,1:T(8,128)} async-done(((f32[64,2,5120]{2,0,1:T(8,128)}), f32[8,2,5120]{2,0,1:T(8,128)}) %reduce-scatter.9.cloned.1.call-update) | async-done | bytes 327696 | tf_op jit(solution)/shard_map/reduce_scatter | solution.py:142
  550.1 13.4 %all_to_all.24 = bf16[8,4,5120]{2,1,0:T(4,128)(2,1)S(1)} all-to-all(bf16[8,4,5120]{2,1,0:T(4,128)(2,1)S(1)} %all_to_all.16), channel_id=1, replica_groups=mesh['ctx'=16,'exp'=8] {'exp'}, dimensions={0} | all-to-all | bytes 655360 | tf_op jit(solution)/shard_map/all_to_all | solution.py:179
  564.4 56.1 %all-gather.5.cloned.1.call-done = bf16[512,5120]{1,0:T(8,128)(2,1)} async-done(((bf16[32,5120]{1,0:T(8,128)(2,1)}), bf16[512,5120]{1,0:T(8,128)(2,1)}) %all-gather.5.cloned.1.call-update) | async-done | bytes 5242896 | tf_op jit(solution)/shard_map/all_gather | solution.py:180
  620.5 7.1 fusion.45
  637.9 77.8 %reduce-scatter.11.cloned.1.call-done = bf16[32,5120]{1,0:T(8,128)(2,1)} async-done(((bf16[512,5120]{1,0:T(8,128)(2,1)}), bf16[32,5120]{1,0:T(8,128)(2,1)}) %reduce-scatter.11.cloned.1.call-update) | async-done | bytes 327696 | tf_op jit(solution)/shard_map/reduce_scatter | solution.py:187
  716.9 13.3 %all_to_all.25 = bf16[8,4,5120]{2,1,0:T(4,128)(2,1)S(1)} all-to-all(bf16[8,4,5120]{2,1,0:T(4,128)(2,1)S(1)} %all_to_all.19), channel_id=1, replica_groups=mesh['ctx'=16,'exp'=8] {'exp'}, dimensions={0} | all-to-all | bytes 655360 | tf_op jit(solution)/shard_map/all_to_all | solution.py:190
  (183 shorter events, 84.6 us)
Async XLA Ops:
  7.2 539.6 %copy-start = (bf16[5120,8]{0,1:T(8,128)(2,1)S(1)}, bf16[5120,8]{0,1:T(8,128)(2,1)}, u32[]{:S(2)}) copy-start(bf16[5120,8]{0,1:T(8,128)(2,1)} %param.34) | copy-start | bytes 245764
  7.2 52.3 %all-gather.3.cloned.1.call-start = ((), (), s32[]{:S(2)}) async-start(), calls=%async_computation.6 | async-start | bytes 2785280 | tf_op jit(solution)/shard_map/all_gather | solution.py:98
  8.9 415.9 %reduce-scatter.13.cloned.1.call-start = ((), (), s32[]{:S(2)}) async-start(), calls=%async_computation.11 | async-start | bytes 557056
  11.2 59.7 %copy-start.4 = (bf16[64,128]{1,0:T(8,128)(2,1)S(1)}, bf16[64,128]{1,0:T(8,128)(2,1)}, u32[]{:S(2)}) copy-start(bf16[64,128]{1,0:T(8,128)(2,1)} %param.25) | copy-start | bytes 49156
  11.2 59.7 %copy-start.5 = (bf16[64,128]{1,0:T(8,128)(2,1)S(1)}, bf16[64,128]{1,0:T(8,128)(2,1)}, u32[]{:S(2)}) copy-start(bf16[64,128]{1,0:T(8,128)(2,1)} %param.26) | copy-start | bytes 49156
  343.2 164.4 %reduce-scatter.7.cloned.1.call-start = ((), (), s32[]{:S(2)}) async-start(), calls=%async_computation.7 | async-start | bytes 5570560 | tf_op jit(solution)/shard_map/reduce_scatter | solution.py:120
  359.3 0.9 copy-start.6
  359.3 1.0 copy-start.7
  359.3 1.2 copy-start.8
  359.3 186.3 %reduce-scatter.9.cloned.1.call-start = ((), (), s32[]{:S(2)}) async-start(), calls=%async_computation.8 | async-start | bytes 2949120 | tf_op jit(solution)/shard_map/reduce_scatter | solution.py:142
  427.0 86.3 %copy-start.9 = (bf16[5120]{0:T(1024)(128)(2,1)S(1)}, bf16[5120]{0:T(1024)(128)(2,1)}, u32[]{:S(2)}) copy-start(bf16[5120]{0:T(1024)(128)(2,1)} %param.33) | copy-start | bytes 30724
  427.1 86.3 %copy-start.10 = (s32[8,1]{0,1:T(1,128)S(1)}, s32[8,1]{0,1:T(1,128)}, u32[]{:S(2)}) copy-start(s32[8,1]{0,1:T(1,128)} %param.36) | copy-start | bytes 100
  427.1 86.3 %copy-start.11 = (s32[8,1]{0,1:T(1,128)S(1)}, s32[8,1]{0,1:T(1,128)}, u32[]{:S(2)}) copy-start(s32[8,1]{0,1:T(1,128)} %param.35) | copy-start | bytes 100
  427.1 118.5 %copy-start.2 = (bf16[8,5120]{1,0:T(8,128)(2,1)S(1)}, bf16[8,5120]{1,0:T(8,128)(2,1)}, u32[]{:S(2)}) copy-start(bf16[8,5120]{1,0:T(8,128)(2,1)} %param.32) | copy-start | bytes 245764
  427.1 118.5 %copy-start.3 = (bf16[8,5120]{1,0:T(8,128)(2,1)S(1)}, bf16[8,5120]{1,0:T(8,128)(2,1)}, u32[]{:S(2)}) copy-start(bf16[8,5120]{1,0:T(8,128)(2,1)} %param.31) | copy-start | bytes 245764
  513.3 107.2 %all-gather.5.cloned.1.call-start = ((), (), s32[]{:S(2)}) async-start(), calls=%async_computation.9 | async-start | bytes 5570560 | tf_op jit(solution)/shard_map/all_gather | solution.py:180
  564.3 151.5 %reduce-scatter.11.cloned.1.call-start = ((), (), s32[]{:S(2)}) async-start(), calls=%async_computation.10 | async-start | bytes 5570560 | tf_op jit(solution)/shard_map/reduce_scatter | solution.py:187
  620.5 7.1 copy-start.12
  620.5 12.7 %slice-start = ((s8[5242880]{0:T(1024)(128)(4,1)}), s8[4194304]{0:T(1024)(128)(4,1)S(1)}, s32[]{:S(2)}) async-start(s8[5242880]{0:T(1024)(128)(4,1)} %bitcast.199), calls=%async_computation.12 | async-start | bytes 8388608
  627.6 5.6 slice-start.1
  637.9 92.4 %copy-start.1 = (f32[8,2,5120]{2,0,1:T(8,128)S(1)}, f32[8,2,5120]{2,0,1:T(8,128)}, u32[]{:S(2)}) copy-start(f32[8,2,5120]{2,0,1:T(8,128)} %reduce-scatter.9.cloned.1.call-done) | copy-start | bytes 983044
Sparse Core Ops, SparseCore 0:
  10.2 49.3 all-gather.2
  343.3 81.3 reduce-scatter.12
  428.5 79.0 reduce-scatter.6
  513.4 32.1 reduce-scatter.8
  564.4 56.0 all-gather.4
  638.1 77.6 reduce-scatter.10
where the time goes:
time: 740 us; the launch traced here: 738 us
  waiting for transfers between devices  359 us (49%)
  matrix products  145 us (20%)
  blocking collectives  84.9 us (11%)
  other arithmetic  77.5 us (10%)
  local copies, waits for them, and re-layouts  48.7 us (7%)
  between operations  14.5 us (2%)
  loops' own time  8.13 us (1%)
    reduce_scatter x1, waiting for transfers between devices, on_device(): lax.psum_scatter(scaled_numer, 'ctx', scatter_dimension=0, tiled=True)  80.5 us
    reduce_scatter x1, waiting for transfers between devices, on_device(): lax.psum_scatter(partial_out.astype(jnp.float32).astype(jnp.bfloat16), 'c...  77.8 us
    unnamed x7, waiting for transfers between devices  64.3 us
    reduce_sum x8, other arithmetic, attend_block(): denom_part = jnp.sum(weight_pre, -1) + jnp.sum(weight_span, -1)  61.1 us
    pmax x1, blocking collectives, on_device(): top_every = lax.pmax(top_max, 'ctx')  58.2 us
    dot_general x4, matrix products, attend_block(): jnp.einsum('bskgd,jkd->bskgj', queries, key_pre, preferred_element_type=j...  57.6 us
    all_gather x1, waiting for transfers between devices, on_device(): shard_rows = lax.all_gather(arrived, 'ctx', axis=0, tiled=True)  56.1 us
    dot_general x4, matrix products, attend_block(): jnp.einsum('bskgj,jkd->bskgd', weight_pre.astype(jnp.bfloat16), val_pre,...  55.1 us
  transfers between devices with their start and end apart: 6, of which 6 were waited for; matrix products, arithmetic and copies ran while one was open for 3% of the time, Pallas kernels for 0%

commit v1 on v0

v1 whole, which is shorter than its diff:
```python
import functools

import jax
import jax.numpy as jnp
from jax import lax
from jax.experimental import pallas as pl
from jax.experimental.pallas import tpu as pltpu
from jax.sharding import PartitionSpec as P

HEAD = 128
NEG = -1e30
EPS = 1e-05
SCALE2 = HEAD ** (-0.5) * 1.4426950408889634
NY = 4
NZ = 4
N_CTX = NY * NZ
N_X = 4
N_EXP = 2 * N_X
KEY_TILE = 512
MESH = pl.DeviceIdType.MESH
BF16 = jnp.bfloat16
F32 = jnp.float32


def copy_to(src, dst, send_sem, recv_sem, **where):
    return pltpu.make_async_remote_copy(
        src_ref=src,
        dst_ref=dst,
        send_sem=send_sem,
        recv_sem=recv_sem,
        device_id=where,
        device_id_type=MESH,
    )


def attention_kernel(
    sq_ref, dq_ref, pos_ref, k_ref, v_ref, sk_ref, sv_ref, dk_ref, dv_ref,
    attn_ref,
    qbuf, kx, vx, num_out, stat_out, num_in, stat_in,
    q_send, q_recv, n_send, n_recv, s_send, s_recv,
):
    tok = sq_ref.shape[0]
    heads = sq_ref.shape[1] // HEAD
    pre = k_ref.shape[0]
    me = lax.axis_index("ctx")
    my_y, my_z = me // NZ, me % NZ

    def offset(k):
        off = (5 * k) % N_CTX
        return off // NZ, off % NZ

    def ahead(k):
        dy, dz = offset(k)
        return ((my_y + dy) % NY) * NZ + (my_z + dz) % NZ

    def behind(k):
        dy, dz = offset(k)
        return ((my_y + NY - dy) % NY) * NZ + (my_z + NZ - dz) % NZ

    barrier = pltpu.get_barrier_semaphore()
    for k in range(1, N_CTX):
        pl.semaphore_signal(barrier, inc=1, device_id={"ctx": ahead(k)}, device_id_type=MESH)
    qbuf[me, :tok] = sq_ref[...]
    qbuf[me, tok:] = dq_ref[...]
    kx[:pre] = k_ref[...]
    kx[pre : pre + tok] = sk_ref[...]
    kx[pre + tok :] = jnp.zeros((kx.shape[0] - pre - tok, HEAD), BF16)
    vx[:pre, :HEAD] = v_ref[...]
    vx[pre : pre + tok, :HEAD] = sv_ref[...]
    vx[pre + tok :, :HEAD] = jnp.zeros((kx.shape[0] - pre - tok, HEAD), BF16)
    vx[:, HEAD:] = jnp.ones((vx.shape[0], HEAD), BF16)
    pl.semaphore_wait(barrier, N_CTX - 1)

    def q_copy(k):
        return copy_to(qbuf.at[me], qbuf.at[me], q_send.at[k], q_recv.at[k], ctx=ahead(k))

    def send_q(k, carry):
        q_copy(k).start()
        return carry

    lax.fori_loop(1, N_CTX, send_q, 0)

    def n_copy(k, dst):
        return copy_to(num_out.at[k], num_in.at[k], n_send.at[k], n_recv.at[k], ctx=dst)

    def s_copy(k, dst):
        return copy_to(stat_out.at[k], stat_in.at[k], s_send.at[k], s_recv.at[k], ctx=dst)

    def tile_step(q, lo, hi, mask, state):
        s = lax.dot_general(
            q, kx[lo:hi], (((1,), (1,)), ((), ())), preferred_element_type=F32
        )
        s = mask(s, lo)
        top = jnp.max(s, -1, keepdims=True)
        if state is not None:
            old_top, old = state
            top = jnp.maximum(old_top, top)
        w = jnp.exp2((s - top) * SCALE2).astype(BF16)
        out = jnp.dot(w, vx[lo:hi], preferred_element_type=F32)
        if state is not None:
            out = old * jnp.exp2((old_top - top) * SCALE2) + out
        return top, out

    lane = lax.broadcasted_iota(jnp.int32, (tok, HEAD), 1)

    def block(k, carry):
        src = behind(k)

        @pl.when(k > 0)
        def _():
            q_copy(k).wait_recv()

        row = lax.broadcasted_iota(jnp.int32, (tok, 1), 0)
        span_limit = src * tok + row - me * tok + 1
        span_limit = jnp.clip(span_limit, 0, tok)
        dec_limit = pos_ref[src][:, :1] - me * pre
        stats = []
        for kind in range(2):
            q = qbuf[src, kind * tok : (kind + 1) * tok]
            q = jnp.concatenate([q[:, h * HEAD : (h + 1) * HEAD] for h in range(heads)], 0)
            limit = jnp.concatenate([span_limit if kind == 0 else dec_limit] * heads, 0)

            def mask(s, lo):
                if kind == 0 and lo + s.shape[1] <= pre:
                    return s
                column = lax.broadcasted_iota(jnp.int32, s.shape, 1)
                if kind == 0:
                    hidden_from = limit + (pre - lo)
                else:
                    hidden_from = limit - lo
                return jnp.where(column < hidden_from, s, NEG)

            state = None
            last = pre + (kx.shape[0] - pre if kind == 0 else 0)
            edges = list(range(0, pre, KEY_TILE)) + [last]
            for lo, hi in zip(edges[:-1], edges[1:]):
                state = tile_step(q, lo, hi, mask, state)
            top, out = state
            num = out[:, :HEAD].astype(BF16)
            stat = jnp.zeros((tok, HEAD), F32)
            for h in range(heads):
                rows = slice(h * tok, (h + 1) * tok)
                num_out[k, kind * tok : (kind + 1) * tok, h * HEAD : (h + 1) * HEAD] = num[rows]
                stat = jnp.where(lane == h, top[rows], stat)
                stat = jnp.where(lane == 8 + h, out[rows, HEAD:], stat)
            stats.append(stat)
        stat_out[k] = jnp.concatenate(stats, 0).T[:16]

        @pl.when(k > 0)
        def _():
            n_copy(k, src).start()
            s_copy(k, src).start()

        return carry

    lax.fori_loop(0, N_CTX, block, 0)

    own = []
    for kind in range(2):
        stat = jnp.full((tok, HEAD), NEG, F32)
        if kind == 1:
            key = dk_ref[...].astype(F32)
            for h in range(heads):
                query = dq_ref[:, h * HEAD : (h + 1) * HEAD].astype(F32)
                score = jnp.sum(query * key, -1, keepdims=True)
                stat = jnp.where(lane == h, score, stat)
        own.append(stat)
    own_top = jnp.concatenate(own, 0).T[:8]

    def finish(k, carry):
        q_copy(k).wait_send()
        n_copy(k, ahead(k)).wait()
        s_copy(k, ahead(k)).wait()
        return carry

    lax.fori_loop(1, N_CTX, finish, 0)
    stat_in[0] = stat_out[0]
    num_in[0] = num_out[0]
    total = own_top
    for k in range(N_CTX):
        total = jnp.maximum(total, stat_in[k, :8])
    own_weight = jnp.exp2((own_top - total) * SCALE2)
    denom = own_weight
    weights = []
    for k in range(N_CTX):
        w = jnp.exp2((stat_in[k, :8] - total) * SCALE2)
        denom = denom + w * stat_in[k, 8:16]
        weights.append(w)
    weights = (jnp.concatenate(weights, 0) / jnp.concatenate([denom] * N_CTX, 0)).T
    own_weight = jnp.concatenate([own_weight / denom] * N_CTX, 0).T
    for h in range(heads):
        columns = slice(h * HEAD, (h + 1) * HEAD)
        acc = jnp.zeros((2 * tok, HEAD), F32)
        for k in range(N_CTX):
            acc = acc + weights[:, k * 8 + h : k * 8 + h + 1] * num_in[k, :, columns].astype(F32)
        own_value = own_weight[tok:, h : h + 1] * dv_ref[...].astype(F32)
        attn_ref[:tok, columns] = acc[:tok].astype(BF16)
        attn_ref[tok:, columns] = (acc[tok:] + own_value).astype(BF16)


def expert_kernel(
    attn_ref, sr_ref, dr_ref, gain_ref, router_ref, se_ref, de_ref,
    ow_hbm, wg_hbm, wu_hbm, wd_hbm,
    span_ref, dec_ref,
    ow, wg, wu, wd, cout, cin, xout, xin, stream_ref, norm_ref, mout, min_, xg, hid, po,
    r1, r2, ph, r3, r4, fin, rout, rin,
    w_sem, c_send, c_recv, x_send, x_recv, a_send, a_recv, g_send, g_recv,
    r_send, r_recv, b_send, b_recv,
):
    quarter = xg.shape[-1]
    me_c, me_e = lax.axis_index("ctx"), lax.axis_index("exp")
    my_y, my_z = me_c // NZ, me_c % NZ
    my_x, my_k = me_e // 2, me_e % 2
    tok = attn_ref.shape[0] // 2
    rows = tok // N_EXP
    slots = 4 * N_EXP

    def along(axis, step):
        if axis == 0:
            return ((my_y + step) % NY) * NZ + my_z
        return my_y * NZ + (my_z + step) % NZ

    def load(i, src, dst):
        return pltpu.make_async_copy(src, dst, w_sem.at[i])

    loads = [load(q, ow_hbm.at[:, pl.ds(q * quarter, quarter)], ow.at[q]) for q in range(4)]
    loads += [load(4, wg_hbm.at[0], wg), load(5, wu_hbm.at[0], wu)]
    loads += [load(6 + q, wd_hbm.at[0, :, pl.ds(q * quarter, quarter)], wd.at[q]) for q in range(4)]
    for c in loads:
        c.start()

    barrier = pltpu.get_barrier_semaphore()
    for k in range(1, N_EXP):
        pl.semaphore_signal(
            barrier, inc=1, device_id={"exp": (me_e + k) % N_EXP}, device_id_type=MESH
        )
    for axis in range(2):
        for step in (1, 3):
            pl.semaphore_signal(
                barrier, inc=1, device_id={"ctx": along(axis, step)}, device_id_type=MESH
            )
    pl.semaphore_wait(barrier, N_EXP - 1 + 4)

    other = me_e + 1 - 2 * my_k

    def c_copy(q):
        return copy_to(cout.at[q], cin.at[q], c_send.at[q], c_recv.at[q], exp=other)

    def x_copy(q, step):
        return copy_to(
            xout.at[q, (my_x + step) % N_X], xin.at[q, step - 1],
            x_send.at[q * 3 + step - 1], x_recv.at[q * 3 + step - 1],
            exp=((my_x + step) % N_X) * 2 + my_k,
        )

    for q in range(4):
        loads[q].wait()
        part = jnp.dot(attn_ref[...], ow[q], preferred_element_type=F32)
        for e in range(N_EXP):
            both = jnp.concatenate(
                [part[e * rows : (e + 1) * rows], part[tok + e * rows : tok + (e + 1) * rows]], 0
            )

            @pl.when(my_k == e % 2)
            def _():
                xout[q, e // 2] = both.astype(BF16)

            @pl.when(my_k != e % 2)
            def _():
                cout[q, e // 2] = both.astype(BF16)

        c_copy(q).start()
    for q in range(4):
        c_copy(q).wait_recv()
        xout[q] = (xout[q].astype(F32) + cin[q].astype(F32)).astype(BF16)
        for step in (1, 3, 2):
            x_copy(q, step).start()
    for q in range(4):
        columns = slice(q * quarter, (q + 1) * quarter)
        total = xout[q, my_x].astype(F32)
        for step in (1, 2, 3):
            x_copy(q, step).wait_recv()
            total = total + xin[q, step - 1].astype(F32)
        resid = jnp.concatenate(
            [sr_ref[:, columns].astype(F32), dr_ref[:, columns].astype(F32)], 0
        )
        stream_ref[:, columns] = total + resid

    width = 4 * quarter
    square = jnp.zeros((2 * rows, 1), F32)
    for q in range(4):
        part = stream_ref[:, q * quarter : (q + 1) * quarter]
        square = square + jnp.sum(part * part, -1, keepdims=True)
    inverse = lax.rsqrt(square / width + EPS)
    logits = jnp.zeros((2 * rows, router_ref.shape[1]), F32)
    for q in range(4):
        columns = slice(q * quarter, (q + 1) * quarter)
        normed = (stream_ref[:, columns] * inverse * gain_ref[:, columns].astype(F32)).astype(BF16)
        norm_ref[:, columns] = normed
        logits = logits + jnp.dot(normed, router_ref[columns], preferred_element_type=F32)
    ids = jnp.concatenate([se_ref[...], de_ref[...]], 0)
    e_lane = lax.broadcasted_iota(jnp.int32, logits.shape, 1)
    chosen = ids == e_lane
    gate = jax.nn.sigmoid(jnp.sum(jnp.where(chosen, logits, 0.0), -1, keepdims=True))
    row_a = lax.broadcasted_iota(jnp.int32, (2 * rows, 2 * rows), 0)
    row_b = lax.broadcasted_iota(jnp.int32, (2 * rows, 2 * rows), 1)
    earlier = (row_b < row_a) & ((row_b < rows) == (row_a < rows))
    chosen_f = jnp.where(chosen, 1.0, 0.0)
    counts = jnp.dot(
        jnp.where(earlier, 1.0, 0.0).astype(BF16), chosen_f.astype(BF16),
        preferred_element_type=F32,
    )
    slot = jnp.sum(chosen_f * counts, -1, keepdims=True)
    kind = jnp.where(lax.broadcasted_iota(jnp.int32, (2 * rows, 1), 0) < rows, 0.0, 2.0)
    place = ids.astype(F32) * 16.0 + kind + slot
    place = jnp.concatenate([place + 4.0 * q for q in range(4)], 0)
    m_lane = lax.broadcasted_iota(jnp.int32, (8 * rows, 4 * slots), 1).astype(F32)
    pick = jnp.where(place == m_lane, 1.0, 0.0).astype(BF16)
    routed = jnp.concatenate(
        [
            (norm_ref[:, q * quarter : (q + 1) * quarter].astype(F32) * gate).astype(BF16)
            for q in range(4)
        ],
        0,
    )
    sent = lax.dot_general(
        pick, routed, (((0,), (0,)), ((), ())), preferred_element_type=F32
    ).astype(BF16)
    for e in range(N_EXP):
        mout[e] = sent[e * 16 : (e + 1) * 16]

    def a_copy(k):
        dst = (me_e + k) % N_EXP
        return copy_to(mout.at[dst], min_.at[me_e], a_send.at[k], a_recv.at[k], exp=dst)

    for k in range(1, N_EXP):
        a_copy(k).start()
    min_[me_e] = mout[me_e]
    for k in range(1, N_EXP):
        a_copy(k).wait_recv()

    to_row = lax.broadcasted_iota(jnp.int32, (4 * slots, 4 * slots), 0)
    from_row = lax.broadcasted_iota(jnp.int32, (4 * slots, 4 * slots), 1)
    wanted = (to_row % slots) // 4 * 16 + (to_row // slots) * 4 + to_row % 4
    perm = jnp.where(wanted == from_row, 1.0, 0.0).astype(BF16)
    wanted_back = (to_row % 16) // 4 * slots + (to_row // 16) * 4 + to_row % 4
    perm_back = jnp.where(wanted_back == from_row, 1.0, 0.0).astype(BF16)
    arrived = min_[...].reshape(4 * slots, quarter)
    arrived = jnp.dot(perm, arrived, preferred_element_type=F32).astype(BF16)
    for q in range(4):
        xg[q, my_y, my_z] = arrived[q * slots : (q + 1) * slots]

    def g_block(half, phase, line, step):
        first = 1 - half
        axis = first if phase == 0 else 1 - first
        base = [my_y, my_z]
        if phase == 1:
            base[first] = (base[first] + line) % 4
        base[axis] = (base[axis] + step) % 4
        return axis, base[0], base[1]

    def g_copy(half, phase, line, direction, piece, hop):
        axis, _, _ = g_block(half, phase, line, 0)
        step = 0 if hop == 0 else (3 if direction == 0 else 1)
        _, by, bz = g_block(half, phase, line, step)
        q = 2 * half + piece
        slot_ = 0 if phase == 0 else 1 + line
        index = (half * 5 + slot_) * 6 + (direction * 2 + piece if hop == 0 else 4 + direction)
        return copy_to(
            xg.at[q, by, bz], xg.at[q, by, bz], g_send.at[index], g_recv.at[index],
            ctx=along(axis, 1 if direction == 0 else 3),
        )

    def g_start(half, phase, line):
        for piece in range(2):
            g_copy(half, phase, line, 0, piece, 0).start()
            g_copy(half, phase, line, 1, 1 - piece, 0).start()

    def g_forward(half, phase, line):
        for direction in range(2):
            g_copy(half, phase, line, direction, direction, 0).wait_recv()
            g_copy(half, phase, line, direction, direction, 1).start()

    def g_near(half, phase, line):
        for direction in range(2):
            g_copy(half, phase, line, direction, 1 - direction, 0).wait_recv()

    def g_far(half, phase, line):
        for direction in range(2):
            g_copy(half, phase, line, direction, direction, 1).wait_recv()

    def g_sent(half, phase, line):
        for direction in range(2):
            for piece in range(2):
                g_copy(half, phase, line, direction, piece, 0).wait_send()
            g_copy(half, phase, line, direction, direction, 1).wait_send()

    for half in range(2):
        g_start(half, 0, 0)
    for half in range(2):
        g_start(half, 1, 0)
    for half in range(2):
        g_forward(half, 0, 0)
    for half in range(2):
        g_near(half, 0, 0)
        g_start(half, 1, 1)
        g_start(half, 1, 3)
    for half in range(2):
        g_forward(half, 1, 0)
    for half in range(2):
        g_far(half, 0, 0)
        g_start(half, 1, 2)
    for line in (1, 3, 2):
        for half in range(2):
            g_forward(half, 1, line)
    for line in range(4):
        for half in range(2):
            g_near(half, 1, line)
            g_far(half, 1, line)

    loads[4].wait()
    loads[5].wait()

    def hidden_rows(i, carry):
        gate_h = jnp.zeros((2 * NZ * slots, wg.shape[1]), F32)
        up_h = jnp.zeros((2 * NZ * slots, wg.shape[1]), F32)
        for q in range(4):
            x = xg[q, pl.ds(2 * i, 2)].reshape(2 * NZ * slots, quarter)
            w_rows = slice(q * quarter, (q + 1) * quarter)
            gate_h = gate_h + jnp.dot(x, wg[w_rows], preferred_element_type=F32)
            up_h = up_h + jnp.dot(x, wu[w_rows], preferred_element_type=F32)
        hid[i] = (gate_h / (1.0 + jnp.exp(-gate_h)) * up_h).astype(BF16)
        return carry

    lax.fori_loop(0, 2, hidden_rows, 0)

    def r_line(ref, q, axis, step):
        if axis == 0:
            return ref.at[q, (my_y + step) % NY]
        return ref.at[q, :, (my_z + step) % NZ]

    def r_copy(half, phase, direction, piece, hop):
        axis = half if phase == 0 else 1 - half
        q = 2 * half + piece
        step = 2 if hop == 0 else (1 if direction == 0 else 3)
        index = (half * 2 + phase) * 6 + (4 + direction if hop == 0 else direction * 2 + piece)
        if phase == 0:
            src = r_line(po, q, axis, step)
            dst = r1.at[half, direction] if hop == 0 else r2.at[half, direction, piece]
        else:
            coord = my_y if axis == 0 else my_z
            src = ph.at[q, (coord + step) % 4]
            dst = r3.at[half, direction] if hop == 0 else r4.at[half, direction, piece]
        return copy_to(
            src, dst, r_send.at[index], r_recv.at[index],
            ctx=along(axis, 1 if direction == 0 else 3),
        )

    def r_begin(half, phase):
        for direction in range(2):
            r_copy(half, phase, direction, direction, 0).start()
        for direction in range(2):
            r_copy(half, phase, direction, 1 - direction, 1).start()

    def r_middle(half, phase):
        axis = half if phase == 0 else 1 - half
        for direction in range(2):
            r_copy(half, phase, direction, direction, 0).wait_recv()
            q = 2 * half + direction
            step = 1 if direction == 0 else 3
            if phase == 0:
                line = r_line(po, q, axis, step)
                line[...] = (line[...].astype(F32) + r1[half, direction].astype(F32)).astype(BF16)
            else:
                coord = ((my_y if axis == 0 else my_z) + step) % 4
                ph[q, coord] = (
                    ph[q, coord].astype(F32) + r3[half, direction].astype(F32)
                ).astype(BF16)
            r_copy(half, phase, direction, direction, 1).start()

    def r_finish(half, phase):
        axis = half if phase == 0 else 1 - half
        for direction in range(2):
            for piece in range(2):
                r_copy(half, phase, direction, piece, 1).wait_recv()
        for piece in range(2):
            q = 2 * half + piece
            if phase == 0:
                total = r_line(po, q, axis, 0)[...].astype(F32)
                total = total + r2[half, 0, piece].astype(F32) + r2[half, 1, piece].astype(F32)
                ph[q] = total.astype(BF16)
            else:
                coord = my_y if axis == 0 else my_z
                total = ph[q, coord].astype(F32)
                total = total + r4[half, 0, piece].astype(F32) + r4[half, 1, piece].astype(F32)
                fin[q] = total.astype(BF16)

    def r_sent(half, phase):
        for direction in range(2):
            r_copy(half, phase, direction, direction, 0).wait_send()
            for piece in range(2):
                r_copy(half, phase, direction, piece, 1).wait_send()

    def down(q):
        loads[6 + q].wait()
        for i in range(2):
            part = jnp.dot(hid[i], wd[q], preferred_element_type=F32)
            po[q, 2 * i : 2 * i + 2] = part.astype(BF16).reshape(2, NZ, slots, quarter)

    down(0)
    down(1)
    r_begin(0, 0)
    down(2)
    down(3)
    r_begin(1, 0)
    for half in range(2):
        r_middle(half, 0)
    for half in range(2):
        r_finish(half, 0)
        r_begin(half, 1)
    for half in range(2):
        r_middle(half, 1)
    for half in range(2):
        r_finish(half, 1)

    back = jnp.dot(
        perm_back, fin[...].reshape(4 * slots, quarter), preferred_element_type=F32
    ).astype(BF16)
    for e in range(N_EXP):
        rout[e] = back[e * 16 : (e + 1) * 16]

    def b_copy(k):
        dst = (me_e + k) % N_EXP
        return copy_to(rout.at[dst], rin.at[me_e], b_send.at[k], b_recv.at[k], exp=dst)

    for k in range(1, N_EXP):
        b_copy(k).start()
    rin[me_e] = rout[me_e]
    for k in range(1, N_EXP):
        b_copy(k).wait_recv()
    result = jnp.dot(pick, rin[...].reshape(4 * slots, quarter), preferred_element_type=F32)
    for q in range(4):
        columns = slice(q * quarter, (q + 1) * quarter)
        both = stream_ref[:, columns] + result[q * 2 * rows : (q + 1) * 2 * rows]
        span_ref[:, columns] = both[:rows].astype(BF16)
        dec_ref[:, columns] = both[rows:].astype(BF16)

    for q in range(4):
        c_copy(q).wait_send()
        for step in (1, 2, 3):
            x_copy(q, step).wait_send()
    for k in range(1, N_EXP):
        a_copy(k).wait_send()
        b_copy(k).wait_send()
    for half in range(2):
        g_sent(half, 0, 0)
        for line in range(4):
            g_sent(half, 1, line)
        for phase in range(2):
            r_sent(half, phase)


def on_device(
    span_q, decode_q, k_cache, v_cache, span_k, span_v, decode_k, decode_v, decode_pos,
    out_weight, span_resid, decode_resid, norm_gain, router, span_expert, decode_expert,
    w_gate, w_up, w_down,
):
    tok, width = span_q.shape
    pre = k_cache.shape[0]
    model = out_weight.shape[1]
    hidden = w_gate.shape[2]
    quarter = model // 4
    rows = tok // N_EXP
    slots = 4 * N_EXP
    vmem = pl.BlockSpec(memory_space=pltpu.VMEM)
    hbm = pl.BlockSpec(memory_space=pl.ANY)
    dma = pltpu.SemaphoreType.DMA
    positions = jnp.broadcast_to(decode_pos.reshape(N_CTX, tok, 1), (N_CTX, tok, HEAD))
    attn = pl.pallas_call(
        attention_kernel,
        out_shape=jax.ShapeDtypeStruct((2 * tok, width), BF16),
        in_specs=[vmem] * 9,
        out_specs=vmem,
        scratch_shapes=[
            pltpu.VMEM((N_CTX, 2 * tok, width), BF16),
            pltpu.VMEM((pre + HEAD, HEAD), BF16),
            pltpu.VMEM((pre + HEAD, 2 * HEAD), BF16),
            pltpu.VMEM((N_CTX, 2 * tok, width), BF16),
            pltpu.VMEM((N_CTX, 16, 2 * tok), F32),
            pltpu.VMEM((N_CTX, 2 * tok, width), BF16),
            pltpu.VMEM((N_CTX, 16, 2 * tok), F32),
        ]
        + [dma((N_CTX,))] * 6,
        compiler_params=pltpu.CompilerParams(
            collective_id=0, has_side_effects=True, vmem_limit_bytes=60 * 2**20
        ),
        name="attention",
    )(
        span_q, decode_q, positions, k_cache, v_cache, span_k, span_v, decode_k, decode_v,
    )
    out = jax.ShapeDtypeStruct((rows, model), BF16)
    span_out, decode_out = pl.pallas_call(
        expert_kernel,
        out_shape=(out, out),
        in_specs=[vmem] * 7 + [hbm] * 4,
        out_specs=(vmem, vmem),
        scratch_shapes=[
            pltpu.VMEM((4, width, quarter), BF16),
            pltpu.VMEM((model, hidden), BF16),
            pltpu.VMEM((model, hidden), BF16),
            pltpu.VMEM((4, hidden, quarter), BF16),
            pltpu.VMEM((4, N_X, 2 * rows, quarter), BF16),
            pltpu.VMEM((4, N_X, 2 * rows, quarter), BF16),
            pltpu.VMEM((4, N_X, 2 * rows, quarter), BF16),
            pltpu.VMEM((4, N_X - 1, 2 * rows, quarter), BF16),
            pltpu.VMEM((2 * rows, model), F32),
            pltpu.VMEM((2 * rows, model), BF16),
            pltpu.VMEM((N_EXP, 16, quarter), BF16),
            pltpu.VMEM((N_EXP, 16, quarter), BF16),
            pltpu.VMEM((4, NY, NZ, slots, quarter), BF16),
            pltpu.VMEM((2, 2 * NZ * slots, hidden), BF16),
            pltpu.VMEM((4, NY, NZ, slots, quarter), BF16),
            pltpu.VMEM((2, 2, 4, slots, quarter), BF16),
            pltpu.VMEM((2, 2, 2, 4, slots, quarter), BF16),
            pltpu.VMEM((4, 4, slots, quarter), BF16),
            pltpu.VMEM((2, 2, slots, quarter), BF16),
            pltpu.VMEM((2, 2, 2, slots, quarter), BF16),
            pltpu.VMEM((4, slots, quarter), BF16),
            pltpu.VMEM((N_EXP, 16, quarter), BF16),
            pltpu.VMEM((N_EXP, 16, quarter), BF16),
            dma((10,)),
            dma((4,)), dma((4,)),
            dma((12,)), dma((12,)),
            dma((N_EXP,)), dma((N_EXP,)),
            dma((60,)), dma((60,)),
            dma((24,)), dma((24,)),
            dma((N_EXP,)), dma((N_EXP,)),
        ],
        compiler_params=pltpu.CompilerParams(
            collective_id=1, has_side_effects=True, vmem_limit_bytes=60 * 2**20
        ),
        name="experts",
    )(
        attn, span_resid, decode_resid, norm_gain.reshape(1, model), router,
        span_expert, decode_expert, out_weight, w_gate, w_up, w_down,
    )
    return span_out, decode_out


def solution(mesh):
    rows = P(("ctx", "exp"), None)
    both = P("ctx", "exp")
    in_specs = (
        (both,) * 8
        + (P(), P("exp", None), rows, rows, P(), P(), rows, rows)
        + (P("exp", None, "ctx"), P("exp", None, "ctx"), P("exp", "ctx", None))
    )
    return jax.shard_map(
        on_device, mesh=mesh, in_specs=in_specs, out_specs=(rows, rows), check_vma=False
    )
```

time: 740 us -> 203 us (0.27)
  waiting for transfers between devices: 359 us -> 0 us
  Pallas kernels: 0 us -> 190 us
  matrix products: 145 us -> 0 us
  blocking collectives: 84.9 us -> 0 us
  other arithmetic: 77.5 us -> 0 us
  local copies, waits for them, and re-layouts: 48.7 us -> 11.1 us
  between operations: 14.5 us -> 0.65 us
  loops' own time: 8.13 us -> 0 us
    pallas_call x0 -> x2, Pallas kernels: none -> 190 us  [the longest x1 115 us: on_device(): pl.pallas_call(expert_kernel, out_shape=(out, out), in_specs=[vmem] * 7 +...]
    reduce_scatter x3 -> x0, waiting for transfers between devices: 190 us -> none  [the longest x1 80.5 us: on_device(): lax.psum_scatter(scaled_numer, 'ctx', scatter_dimension=0, tiled=True)]
    dot_general x23 -> x0, matrix products: 145 us -> none  [the longest x4 57.6 us: attend_block(): jnp.einsum('bskgd,jkd->bskgj', queries, key_pre, preferred_element_type=j...]
    all_gather x2 -> x0, waiting for transfers between devices: 104 us -> none  [the longest x1 56.1 us: on_device(): shard_rows = lax.all_gather(arrived, 'ctx', axis=0, tiled=True)]
    unnamed x7 -> x0, waiting for transfers between devices: 64.3 us -> none
    reduce_sum x11 -> x0, other arithmetic: 62.6 us -> none  [the longest x8 61.1 us: attend_block(): denom_part = jnp.sum(weight_pre, -1) + jnp.sum(weight_span, -1)]
    pmax x1 -> x0, blocking collectives: 58.2 us -> none  [on_device(): top_every = lax.pmax(top_max, 'ctx')]
    all_to_all x2 -> x0, blocking collectives: 26.7 us -> none  [the longest x1 13.4 us: on_device(): lax.all_to_all(buffer, 'exp', split_axis=0, concat_axis=0, tiled=True)]
  transfers between devices with their start and end apart: 6 -> 0, of which waited for: 6 -> 0; matrix products, arithmetic and copies ran while one was open for 3% -> 0% of each run, Pallas kernels for 0% -> 0%
where the time goes in v1:
time: 203 us; the launch traced here: 202 us
  Pallas kernels  190 us (94%)
  local copies, waits for them, and re-layouts  11.1 us (5%)
    pallas_call x1, Pallas kernels, on_device(): pl.pallas_call(expert_kernel, out_shape=(out, out), in_specs=[vmem] * 7 +...  115 us
    pallas_call x1, Pallas kernels, on_device(): pl.pallas_call(attention_kernel, out_shape=jax.ShapeDtypeStruct((2 * tok,...  75.9 us
    unnamed x5, local copies, waits for them, and re-layouts  8.07 us

profile of v1, /device:TPU:1, one launch (start us, length us, event | category | flops | bytes accessed | tf_op | source)
XLA Modules:
  0.0 202.2 jit_solution(17692391725925392475)
XLA Ops:
  0.6 1.3 copy.22.se_ref
  2.0 1.3 copy.23.de_ref
  3.3 0.8 broadcast_in_dim.7
  4.0 1.3 reshape.9.gain_ref
  5.3 1.0 broadcast_in_dim.8.pos_ref
  6.3 75.9 %attention.1.attn_ref = bf16[128,640]{1,0:T(8,128)(2,1)} custom-call(bf16[64,640]{1,0:T(8,128)(2,1)} %sq_ref.1, bf16[64,640]{1,0:T(8,128)(2,1)} %dq_ref.1, s32[16,64,128]{2,1,0:T(8,128)} %broadcast_in_dim.8.pos_ref, bf16[3072,128]{1,0:T(8,128)(2,1)} %k_ref.1, bf16[3072,128]{1,0:T(8,128)(2,1)} %v_ref.1, bf16[64,128]{1,0:T(8,128)(2,1)} %sk_ref.1, ...), custom_call_target="tpu_custom_call" | custom-call | tf_op jit(solution)/shard_map/attention/pallas_call | solution.py:579
  82.2 2.4 %copy.21.router_ref = bf16[5120,8]{1,0:T(8,128)(2,1)} copy(bf16[5120,8]{0,1:T(8,128)(2,1)} %param.32) | data formatting | bytes 163840 | tf_op args[13]
  84.6 114.6 %experts.1 = (bf16[8,5120]{1,0:T(8,128)(2,1)}, bf16[8,5120]{1,0:T(8,128)(2,1)}) custom-call(bf16[128,640]{1,0:T(8,128)(2,1)} %attention.1.attn_ref, bf16[8,5120]{1,0:T(8,128)(2,1)} %sr_ref.1, bf16[8,5120]{1,0:T(8,128)(2,1)} %dr_ref.1, bf16[1,5120]{1,0:T(2,128)(2,1)} %reshape.9.gain_ref, bf16[5120,8]{1,0:T(8,128)(2,1)} %copy.21.router_ref, ...), custom_call_target="tpu_custom_call" | custom-call | tf_op jit(solution)/shard_map/experts/pallas_call | solution.py:602
  199.2 1.5 copy.26
  200.7 1.5 copy.27

commit v2 on v0

v2 whole, which is shorter than its diff:
```python
import functools

import jax
import jax.numpy as jnp
from jax import lax
from jax.experimental import pallas as pl
from jax.experimental.pallas import tpu as pltpu
from jax.sharding import PartitionSpec as P

HEAD = 128
NEG = -1e30
EPS = 1e-05
SCALE2 = HEAD ** (-0.5) * 1.4426950408889634
NY = 4
NZ = 4
N_CTX = NY * NZ
N_X = 4
N_EXP = 2 * N_X
KEY_TILE = 512
MESH = pl.DeviceIdType.MESH
BF16 = jnp.bfloat16
F32 = jnp.float32


def copy_to(src, dst, send_sem, recv_sem, **where):
    return pltpu.make_async_remote_copy(
        src_ref=src,
        dst_ref=dst,
        send_sem=send_sem,
        recv_sem=recv_sem,
        device_id=where,
        device_id_type=MESH,
    )


class Ring:
    def __init__(self, ref, first, here, along, send, recv, base):
        self.ref, self.first, self.here, self.along = ref, first, here, along
        self.send, self.recv, self.base = send, recv, base

    def copy(self, phase, line, direction, piece, hop):
        axis = self.first if phase == 0 else 1 - self.first
        at = list(self.here)
        at[self.first] = (at[self.first] + line) % 4
        step = 0 if hop == 0 else (3 if direction == 0 else 1)
        at[axis] = (at[axis] + step) % 4
        index = self.base + (0 if phase == 0 else 1 + line) * 6
        index = index + (direction * 2 + piece if hop == 0 else 4 + direction)
        block = self.ref(piece, at[0], at[1])
        to = self.along(axis, 1 if direction == 0 else 3)
        return copy_to(block, block, self.send.at[index], self.recv.at[index], ctx=to)

    def start(self, phase, line):
        for piece in range(2):
            self.copy(phase, line, 0, piece, 0).start()
            self.copy(phase, line, 1, 1 - piece, 0).start()

    def forward(self, phase, line):
        for direction in range(2):
            self.copy(phase, line, direction, direction, 0).wait_recv()
            self.copy(phase, line, direction, direction, 1).start()

    def near(self, phase, line):
        for direction in range(2):
            self.copy(phase, line, direction, 1 - direction, 0).wait_recv()

    def far(self, phase, line):
        for direction in range(2):
            self.copy(phase, line, direction, direction, 1).wait_recv()

    def sent(self, phase, line):
        for direction in range(2):
            for piece in range(2):
                self.copy(phase, line, direction, piece, 0).wait_send()
            self.copy(phase, line, direction, direction, 1).wait_send()

    def all_sent(self):
        self.sent(0, 0)
        for line in range(4):
            self.sent(1, line)


def layer_kernel(
    sq_ref, dq_ref, pos_ref, sk_ref, sv_ref, dk_ref, dv_ref, sr_ref, dr_ref, gain_ref,
    router_ref, se_ref, de_ref, k_hbm, v_hbm, ow_hbm, wg_hbm, wu_hbm, wd_hbm,
    span_ref, dec_ref,
    qb, kx, vx, pos_cols, num_out, stat_out, num_in, stat_in, mid_out, mid_stat, last_in,
    last_stat, attn, ow, wg, wu, wd, cout, cin, xout, xin, stream_ref, pick_ref, mout, min_,
    xg, po, r1, r2, ph, r3, r4, fin, rout, rin,
    w_sem, q_send, q_recv, n_send, n_recv, s_send, s_recv, l_send, l_recv, t_send, t_recv,
    c_send, c_recv, x_send, x_recv, a_send, a_recv, g_send, g_recv, r_send, r_recv,
    b_send, b_recv,
):
    me_c, me_e = lax.axis_index("ctx"), lax.axis_index("exp")
    here = (me_c // NZ, me_c % NZ)
    my_y, my_z = here
    my_x, my_k = me_e // 2, me_e % 2
    tok = sq_ref.shape[0]
    heads = sq_ref.shape[1] // HEAD
    pre = k_hbm.shape[0]
    piece_w = xg.shape[-1]
    rows = tok // N_EXP

    def along(axis, step):
        if axis == 0:
            return ((my_y + step) % NY) * NZ + my_z
        return my_y * NZ + (my_z + step) % NZ

    barrier = pltpu.get_barrier_semaphore()
    for k in range(1, N_EXP):
        pl.semaphore_signal(
            barrier, inc=1, device_id={"exp": (me_e + k) % N_EXP}, device_id_type=MESH
        )
    for axis in range(2):
        for step in range(1, 4):
            pl.semaphore_signal(
                barrier, inc=1, device_id={"ctx": along(axis, step)}, device_id_type=MESH
            )

    def load(i, src, dst):
        return pltpu.make_async_copy(src, dst, w_sem.at[i])

    quarter = 2 * piece_w
    loads = [load(0, k_hbm, kx.at[pl.ds(0, pre)])]
    loads += [load(1, v_hbm, vx.at[pl.ds(0, pre), pl.ds(0, HEAD)])]
    loads += [load(2 + q, ow_hbm.at[:, pl.ds(q * quarter, quarter)], ow.at[q]) for q in range(4)]
    loads += [load(6, wg_hbm.at[0], wg), load(7, wu_hbm.at[0], wu)]
    loads += [load(8 + q, wd_hbm.at[0, :, pl.ds(q * quarter, quarter)], wd.at[q]) for q in range(4)]
    for c in loads:
        c.start()

    for kind, ref in enumerate((sq_ref, dq_ref)):
        for piece in range(2):
            half = tok // 2
            qb[kind, my_y, my_z, piece] = ref[piece * half : (piece + 1) * half]
    q_rings = [
        Ring(
            lambda piece, y, z, kind=kind: qb.at[kind, y, z, piece],
            1 - kind, here, along, q_send, q_recv, 30 * kind,
        )
        for kind in range(2)
    ]
    pl.semaphore_wait(barrier, N_EXP - 1 + 6)
    q_rings[0].start(0, 0)
    q_rings[0].start(1, 0)

    extra = kx.shape[0] - pre - tok
    kx[pre : pre + tok] = sk_ref[...]
    kx[pre + tok :] = jnp.zeros((extra, HEAD), BF16)
    vx[pre : pre + tok, :HEAD] = sv_ref[...]
    vx[pre + tok :, :HEAD] = jnp.zeros((extra, HEAD), BF16)
    vx[:, HEAD:] = jnp.ones((vx.shape[0], HEAD), BF16)
    pos_f = pos_ref[...].astype(F32)
    pos_f = jnp.concatenate(
        [pos_f, jnp.zeros((HEAD - pos_f.shape[0], HEAD), F32)], 0
    ).T.astype(jnp.int32)
    for b in range(N_CTX):
        start = (b * tok) % HEAD
        column = (b * tok) // HEAD
        pos_cols[b] = jnp.broadcast_to(
            pos_f[start : start + tok, column : column + 1], (tok, HEAD)
        )
    loads[0].wait()
    loads[1].wait()

    lane = lax.broadcasted_iota(jnp.int32, (tok, HEAD), 1)

    def order(k):
        later = (k + 1) % N_CTX
        group, j = later // 4, later % 4
        j = (j + 3 * ((4 - group) // 4)) % 4
        line = (3 * group + 3 * (group * (group - 1) // 2)) % 4
        step = (3 * j + 3 * (j * (j - 1) // 2)) % 4
        return line, step

    def n_copy(kind, line, step):
        index = kind * 12 + line * 3 + step - 1
        to = along(1 - kind, step)
        return (
            copy_to(
                num_out.at[kind, line, step], num_in.at[kind, line, step - 1],
                n_send.at[index], n_recv.at[index], ctx=to,
            ),
            copy_to(
                stat_out.at[kind, line, step], stat_in.at[kind, line, step - 1],
                s_send.at[index], s_recv.at[index], ctx=to,
            ),
        )

    def l_copy(kind, line):
        index = kind * 3 + line - 1
        to = along(kind, line)
        return (
            copy_to(
                mid_out.at[kind, line - 1], last_in.at[kind, line - 1],
                l_send.at[index], l_recv.at[index], ctx=to,
            ),
            copy_to(
                mid_stat.at[kind, line - 1], last_stat.at[kind, line - 1],
                t_send.at[index], t_recv.at[index], ctx=to,
            ),
        )

    def tile_step(q, lo, hi, mask, state):
        s = lax.dot_general(
            q, kx[lo:hi], (((1,), (1,)), ((), ())), preferred_element_type=F32
        )
        s = mask(s, lo)
        top = jnp.max(s, -1, keepdims=True)
        if state is not None:
            old_top, old = state
            top = jnp.maximum(old_top, top)
        w = jnp.exp2((s - top) * SCALE2).astype(BF16)
        out = jnp.dot(w, vx[lo:hi], preferred_element_type=F32)
        if state is not None:
            out = old * jnp.exp2((old_top - top) * SCALE2) + out
        return top, out

    def attend(kind, k):
        line, step = order(k)
        shift = (line, step) if kind == 0 else (step, line)
        src_y, src_z = (my_y + shift[0]) % NY, (my_z + shift[1]) % NZ
        src = src_y * NZ + src_z
        if kind == 0:
            row = lax.broadcasted_iota(jnp.int32, (tok, 1), 0)
            limit = jnp.clip(src * tok + row - me_c * tok + 1, 0, tok)
        else:
            limit = pos_cols[src][:, :1] - me_c * pre
        q = jnp.concatenate([qb[kind, src_y, src_z, 0], qb[kind, src_y, src_z, 1]], 0)
        q = jnp.concatenate([q[:, h * HEAD : (h + 1) * HEAD] for h in range(heads)], 0)
        limit = jnp.concatenate([limit] * heads, 0)

        def mask(s, lo):
            if kind == 0 and lo + s.shape[1] <= pre:
                return s
            column = lax.broadcasted_iota(jnp.int32, s.shape, 1)
            hidden_from = limit + (pre - lo) if kind == 0 else limit - lo
            return jnp.where(column < hidden_from, s, NEG)

        state = None
        last = kx.shape[0] if kind == 0 else pre
        edges = list(range(0, pre, KEY_TILE)) + [last]
        for lo, hi in zip(edges[:-1], edges[1:]):
            state = tile_step(q, lo, hi, mask, state)
        top, out = state
        num = out[:, :HEAD].astype(BF16)
        stat = jnp.zeros((tok, HEAD), F32)
        for h in range(heads):
            part = slice(h * tok, (h + 1) * tok)
            num_out[kind, line, step, :, h * HEAD : (h + 1) * HEAD] = num[part]
            stat = jnp.where(lane == h, top[part], stat)
            stat = jnp.where(lane == 8 + h, out[part, HEAD:], stat)
        stat = jnp.concatenate([stat, jnp.zeros((HEAD - tok, HEAD), F32)], 0)
        stat_out[kind, line, step] = stat.T[:16]

        @pl.when(step != 0)
        def _():
            for c in n_copy(kind, line, step):
                c.start()

    def merge(parts, own=None):
        top = parts[0][1][:8]
        for _, stat in parts[1:]:
            top = jnp.maximum(top, stat[:8])
        if own is not None:
            top = jnp.maximum(top, own[0])
        weights = [jnp.exp2((stat[:8] - top) * SCALE2) for _, stat in parts]
        denom = weights[0] * parts[0][1][8:]
        for w, (_, stat) in zip(weights[1:], parts[1:]):
            denom = denom + w * stat[8:]
        if own is not None:
            own_w = jnp.exp2((own[0] - top) * SCALE2)
            denom = denom + own_w
            weights = [w / denom for w in weights + [own_w]]
        blank = jnp.zeros((HEAD - 8 * len(weights), HEAD), F32)
        weights = jnp.concatenate(weights + [blank], 0).T
        out = []
        for h in range(heads):
            columns = slice(h * HEAD, (h + 1) * HEAD)
            acc = jnp.zeros((tok, HEAD), F32)
            for i, (num, _) in enumerate(parts):
                acc = acc + weights[:tok, i * 8 + h : i * 8 + h + 1] * num[:, columns].astype(F32)
            if own is not None:
                i = len(parts)
                acc = acc + weights[:tok, i * 8 + h : i * 8 + h + 1] * own[1]
            out.append(acc.astype(BF16))
        return jnp.concatenate(out, 1), jnp.concatenate([top, denom], 0)

    def line_parts(kind, line):
        parts = [(num_out.at[kind, line, 0], stat_out[kind, line, 0])]
        for step in range(1, 4):
            for c in n_copy(kind, line, step):
                c.wait_recv()
            parts.append((num_in.at[kind, line, step - 1], stat_in[kind, line, step - 1]))
        return parts

    def merge_line(kind, line):
        num, stat = merge(line_parts(kind, line))
        mid_out[kind, line - 1] = num
        mid_stat[kind, line - 1] = stat
        for c in l_copy(kind, line):
            c.start()

    def merge_rows(kind):
        parts = line_parts(kind, 0)
        for line in range(1, 4):
            for c in l_copy(kind, line):
                c.wait_recv()
            parts.append((last_in.at[kind, line - 1], last_stat[kind, line - 1]))
        top = jnp.full((8, HEAD), NEG, F32)
        value = jnp.zeros((tok, HEAD), F32)
        if kind == 1:
            key = dk_ref[...].astype(F32)
            value = dv_ref[...].astype(F32)
            stat = jnp.full((tok, HEAD), NEG, F32)
            for h in range(heads):
                query = dq_ref[:, h * HEAD : (h + 1) * HEAD].astype(F32)
                stat = jnp.where(lane == h, jnp.sum(query * key, -1, keepdims=True), stat)
            stat = jnp.concatenate([stat, jnp.full((HEAD - tok, HEAD), NEG, F32)], 0)
            top = stat.T[:8]
        num, _ = merge(parts, (top, value))
        attn[kind] = num

    def c_copy(kind, q):
        i = kind * 4 + q
        return copy_to(
            cout.at[kind, q], cin.at[kind, q], c_send.at[i], c_recv.at[i],
            exp=me_e + 1 - 2 * my_k,
        )

    def x_copy(kind, q, step):
        i = kind * 12 + q * 3 + step - 1
        to = (my_x + step) % N_X
        return copy_to(
            xout.at[kind, q, to], xin.at[kind, q, step - 1], x_send.at[i], x_recv.at[i],
            exp=to * 2 + my_k,
        )

    def project(kind):
        for q in range(4):
            if kind == 0:
                loads[2 + q].wait()
            part = jnp.dot(attn[kind], ow[q], preferred_element_type=F32)
            for e in range(N_EXP):
                own = part[e * rows : (e + 1) * rows]
                own = jnp.concatenate([own[:, :piece_w], own[:, piece_w:]], 0).astype(BF16)

                @pl.when(my_k == e % 2)
                def _():
                    xout[kind, q, e // 2] = own

                @pl.when(my_k != e % 2)
                def _():
                    cout[kind, q, e // 2] = own

            c_copy(kind, q).start()

    def chip_sum(kind):
        for q in range(4):
            c_copy(kind, q).wait_recv()
            xout[kind, q] = (xout[kind, q].astype(F32) + cin[kind, q].astype(F32)).astype(BF16)
            for step in (2, 1, 3):
                x_copy(kind, q, step).start()

    def a_copy(kind, k):
        to = (me_e + k) % N_EXP
        i = kind * N_EXP + k
        return copy_to(
            mout.at[kind, to], min_.at[kind, me_e], a_send.at[i], a_recv.at[i], exp=to
        )

    def b_copy(kind, k):
        to = (me_e + k) % N_EXP
        i = kind * N_EXP + k
        return copy_to(
            rout.at[kind, to], rin.at[kind, me_e], b_send.at[i], b_recv.at[i], exp=to
        )

    def route(kind):
        resid_ref, id_ref = (sr_ref, se_ref) if kind == 0 else (dr_ref, de_ref)
        square = jnp.zeros((rows, 1), F32)
        pieces = []
        for q in range(4):
            total = xout[kind, q, my_x].astype(F32)
            for step in (1, 2, 3):
                x_copy(kind, q, step).wait_recv()
                total = total + xin[kind, q, step - 1].astype(F32)
            for i in range(2):
                columns = slice((2 * q + i) * piece_w, (2 * q + i + 1) * piece_w)
                part = total[i * rows : (i + 1) * rows] + resid_ref[:, columns].astype(F32)
                stream_ref[kind, :, columns] = part
                square = square + jnp.sum(part * part, -1, keepdims=True)
                pieces.append(part)
        inverse = lax.rsqrt(square / (8 * piece_w) + EPS)
        logits = jnp.zeros((rows, N_EXP), F32)
        normed = []
        for i, part in enumerate(pieces):
            columns = slice(i * piece_w, (i + 1) * piece_w)
            part = (part * inverse * gain_ref[:, columns].astype(F32)).astype(BF16)
            normed.append(part)
            logits = logits + lax.dot_general(
                part, router_ref[:, columns], (((1,), (1,)), ((), ())),
                preferred_element_type=F32,
            )
        a = lax.broadcasted_iota(jnp.int32, (rows, N_EXP), 0)
        b = lax.broadcasted_iota(jnp.int32, (rows, N_EXP), 1)
        ids = jnp.sum(jnp.where(a == b, id_ref[...].astype(F32), 0.0), -1, keepdims=True)
        chosen = ids == b.astype(F32)
        gate = jax.nn.sigmoid(jnp.sum(jnp.where(chosen, logits, 0.0), -1, keepdims=True))
        chosen = jnp.where(chosen, 1.0, 0.0)
        counts = jnp.dot(
            jnp.where(b < a, 1.0, 0.0), chosen, preferred_element_type=F32
        )
        slot = jnp.sum(chosen * counts, -1, keepdims=True)
        place = ids * 16.0 + slot
        place = jnp.concatenate([place + 2.0 * i for i in range(8)], 0)
        m_lane = lax.broadcasted_iota(jnp.int32, (8 * rows, 16 * N_EXP), 1).astype(F32)
        pick = jnp.where(place == m_lane, 1.0, 0.0).astype(BF16)
        pick_ref[kind] = pick
        routed = jnp.concatenate([part.astype(F32) * gate for part in normed], 0).astype(BF16)
        sent = lax.dot_general(
            pick, routed, (((0,), (0,)), ((), ())), preferred_element_type=F32
        ).astype(BF16)
        for e in range(N_EXP):
            mout[kind, e] = sent[e * 16 : (e + 1) * 16]
        for k in range(1, N_EXP):
            a_copy(kind, k).start()
        min_[kind, me_e] = mout[kind, me_e]

    def swap():
        n = 16 * N_EXP
        to_row = lax.broadcasted_iota(jnp.int32, (n, n), 0)
        from_row = lax.broadcasted_iota(jnp.int32, (n, n), 1)
        wanted = (to_row % 16) // 2 * 16 + (to_row // 16) * 2 + to_row % 2
        return jnp.where(wanted == from_row, 1.0, 0.0).astype(BF16)

    g_rings = [
        [
            Ring(
                lambda piece, y, z, kind=kind, half=half: xg.at[kind, 2 * half + piece, y, z],
                1 - half, here, along, g_send, g_recv, (kind * 2 + half) * 30,
            )
            for half in range(2)
        ]
        for kind in range(2)
    ]

    def gather_a(kind):
        for k in range(1, N_EXP):
            a_copy(kind, k).wait_recv()
        arrived = min_[kind].reshape(16 * N_EXP, piece_w)
        arrived = jnp.dot(swap(), arrived, preferred_element_type=F32).astype(BF16)
        for i in range(8):
            xg[kind, i // 2, my_y, my_z, i % 2] = arrived[i * 16 : (i + 1) * 16]
        for ring in g_rings[kind]:
            ring.start(0, 0)
        for ring in g_rings[kind]:
            ring.start(1, 0)

    def gather_b(kind):
        for ring in g_rings[kind]:
            ring.forward(0, 0)
        for ring in g_rings[kind]:
            ring.near(0, 0)
            ring.start(1, 1)
            ring.start(1, 3)

    def gather_c(kind):
        for ring in g_rings[kind]:
            ring.forward(1, 0)
        for ring in g_rings[kind]:
            ring.far(0, 0)
            ring.start(1, 2)

    def gather_d(kind):
        for line in (1, 3):
            for ring in g_rings[kind]:
                ring.forward(1, line)

    def gather_e(kind):
        for ring in g_rings[kind]:
            ring.forward(1, 2)

    def r_line(kind, q, axis, step):
        if axis == 0:
            return po.at[kind, q, (my_y + step) % NY]
        return po.at[kind, q, :, (my_z + step) % NZ]

    def r_copy(kind, half, phase, direction, piece, hop):
        axis = half if phase == 0 else 1 - half
        q = 2 * half + piece
        step = 2 if hop == 0 else (1 if direction == 0 else 3)
        index = (kind * 4 + half * 2 + phase) * 6
        index = index + (4 + direction if hop == 0 else direction * 2 + piece)
        if phase == 0:
            src = r_line(kind, q, axis, step)
            dst = r1.at[kind, half, direction] if hop == 0 else r2.at[kind, half, direction, piece]
        else:
            src = ph.at[kind, q, (here[axis] + step) % 4]
            dst = r3.at[kind, half, direction] if hop == 0 else r4.at[kind, half, direction, piece]
        return copy_to(
            src, dst, r_send.at[index], r_recv.at[index],
            ctx=along(axis, 1 if direction == 0 else 3),
        )

    def r_begin(kind, half, phase):
        for direction in range(2):
            r_copy(kind, half, phase, direction, direction, 0).start()
        for direction in range(2):
            r_copy(kind, half, phase, direction, 1 - direction, 1).start()

    def r_middle(kind, half, phase):
        axis = half if phase == 0 else 1 - half
        for direction in range(2):
            r_copy(kind, half, phase, direction, direction, 0).wait_recv()
            q = 2 * half + direction
            step = 1 if direction == 0 else 3
            if phase == 0:
                line, arrived = r_line(kind, q, axis, step), r1.at[kind, half, direction]
            else:
                line, arrived = ph.at[kind, q, (here[axis] + step) % 4], r3.at[kind, half, direction]
            line[...] = (line[...].astype(F32) + arrived[...].astype(F32)).astype(BF16)
            r_copy(kind, half, phase, direction, direction, 1).start()

    def r_finish(kind, half, phase):
        axis = half if phase == 0 else 1 - half
        for direction in range(2):
            for piece in range(2):
                r_copy(kind, half, phase, direction, piece, 1).wait_recv()
        for piece in range(2):
            q = 2 * half + piece
            if phase == 0:
                own, arrived = r_line(kind, q, axis, 0), r2
            else:
                own, arrived = ph.at[kind, q, here[axis]], r4
            total = own[...].astype(F32)
            for direction in range(2):
                total = total + arrived[kind, half, direction, piece].astype(F32)
            if phase == 0:
                ph[kind, q] = total.astype(BF16)
            else:
                fin[kind, q] = total.astype(BF16)

    def experts(kind):
        for line in range(4):
            for ring in g_rings[kind]:
                ring.near(1, line)
                ring.far(1, line)
        if kind == 0:
            loads[6].wait()
            loads[7].wait()
        n = N_CTX * 16
        gate_h = jnp.zeros((n, wg.shape[1]), F32)
        up_h = jnp.zeros((n, wg.shape[1]), F32)
        for q in range(4):
            x = jnp.concatenate(
                [xg[kind, q, :, :, i].reshape(n, piece_w) for i in range(2)], 1
            )
            w_rows = slice(q * quarter, (q + 1) * quarter)
            gate_h = gate_h + jnp.dot(x, wg[w_rows], preferred_element_type=F32)
            up_h = up_h + jnp.dot(x, wu[w_rows], preferred_element_type=F32)
        hidden = (gate_h / (1.0 + jnp.exp(-gate_h)) * up_h).astype(BF16)
        for q in range(4):
            if kind == 0:
                loads[8 + q].wait()
            part = jnp.dot(hidden, wd[q], preferred_element_type=F32).astype(BF16)
            for i in range(2):
                po[kind, q, :, :, i] = part[:, i * piece_w : (i + 1) * piece_w].reshape(
                    NY, NZ, 16, piece_w
                )
            if q % 2 == 1:
                r_begin(kind, q // 2, 0)

    def sums_b(kind):
        for half in range(2):
            r_middle(kind, half, 0)

    def sums_c(kind):
        for half in range(2):
            r_finish(kind, half, 0)
            r_begin(kind, half, 1)

    def sums_d(kind):
        for half in range(2):
            r_middle(kind, half, 1)

    def give_back(kind):
        for half in range(2):
            r_finish(kind, half, 1)
        back = jnp.dot(
            swap(), fin[kind].reshape(16 * N_EXP, piece_w), preferred_element_type=F32
        ).astype(BF16)
        for e in range(N_EXP):
            rout[kind, e] = back[e * 16 : (e + 1) * 16]
        for k in range(1, N_EXP):
            b_copy(kind, k).start()
        rin[kind, me_e] = rout[kind, me_e]

    def write(kind):
        for k in range(1, N_EXP):
            b_copy(kind, k).wait_recv()
        out_ref = span_ref if kind == 0 else dec_ref
        result = jnp.dot(
            pick_ref[kind], rin[kind].reshape(16 * N_EXP, piece_w), preferred_element_type=F32
        )
        for i in range(8):
            columns = slice(i * piece_w, (i + 1) * piece_w)
            part = stream_ref[kind, :, columns] + result[i * rows : (i + 1) * rows]
            out_ref[:, columns] = part.astype(BF16)

    qs, qd = q_rings

    def do(f, *args):
        return lambda: f(*args)

    span_steps = {
        0: [do(qs.forward, 0, 0), do(qs.near, 0, 0), do(qs.start, 1, 1), do(qs.start, 1, 3),
            do(qd.start, 0, 0), do(qd.start, 1, 0)],
        1: [do(qs.forward, 1, 0), do(qs.far, 0, 0), do(qs.start, 1, 2), do(qs.forward, 1, 3)],
        2: [do(qs.forward, 1, 1), do(qs.near, 1, 0), do(qd.forward, 0, 0), do(qd.near, 0, 0),
            do(qd.start, 1, 1), do(qd.start, 1, 3)],
        3: [do(qs.forward, 1, 2), do(qs.near, 1, 3), do(qd.forward, 1, 0), do(qd.far, 0, 0),
            do(qd.start, 1, 2)],
        4: [do(qs.near, 1, 1), do(qd.forward, 1, 3), do(qd.forward, 1, 1)],
        5: [do(qs.near, 1, 2), do(qd.forward, 1, 2)],
        8: [do(merge_line, 0, 3), do(qd.near, 1, 0)],
        9: [do(qd.near, 1, 3)],
        10: [do(qs.far, 1, 0), do(qs.far, 1, 3), do(qd.near, 1, 1)],
        11: [do(qs.far, 1, 1), do(qs.far, 1, 2), do(qd.near, 1, 2)],
        12: [do(merge_line, 0, 1)],
        13: [do(qd.far, 1, 0), do(qd.far, 1, 3)],
        14: [do(qd.far, 1, 1), do(qd.far, 1, 2)],
    }
    dec_steps = {
        0: [do(merge_line, 0, 2)],
        2: [do(merge_rows, 0), do(project, 0)],
        4: [do(chip_sum, 0)],
        7: [do(route, 0)],
        8: [do(merge_line, 1, 3)],
        9: [do(gather_a, 0)],
        10: [do(gather_b, 0)],
        11: [do(gather_c, 0)],
        12: [do(merge_line, 1, 1), do(gather_d, 0)],
        13: [do(gather_e, 0)],
    }
    tail = [
        do(merge_line, 1, 2), do(experts, 0), do(merge_rows, 1), do(project, 1), do(sums_b, 0),
        do(chip_sum, 1), do(sums_c, 0), do(route, 1), do(sums_d, 0), do(gather_a, 1),
        do(give_back, 0), do(gather_b, 1), do(gather_c, 1), do(gather_d, 1), do(write, 0),
        do(gather_e, 1), do(experts, 1), do(sums_b, 1), do(sums_c, 1), do(sums_d, 1),
        do(give_back, 1), do(write, 1),
    ]

    def loop(kind, steps):
        def one(k, carry):
            attend(kind, k)
            for at, actions in steps.items():

                @pl.when(k == at)
                def _():
                    for action in actions:
                        action()

            return carry

        lax.fori_loop(0, N_CTX, one, 0)

    loop(0, span_steps)
    loop(1, dec_steps)
    for action in tail:
        action()

    for kind in range(2):
        q_rings[kind].all_sent()
        for line in range(4):
            for step in range(1, 4):
                for c in n_copy(kind, line, step):
                    c.wait_send()
        for line in range(1, 4):
            for c in l_copy(kind, line):
                c.wait_send()
        for q in range(4):
            c_copy(kind, q).wait_send()
            for step in (1, 2, 3):
                x_copy(kind, q, step).wait_send()
        for k in range(1, N_EXP):
            a_copy(kind, k).wait_send()
            b_copy(kind, k).wait_send()
        for half in range(2):
            g_rings[kind][half].all_sent()
            for phase in range(2):
                for direction in range(2):
                    r_copy(kind, half, phase, direction, direction, 0).wait_send()
                    for piece in range(2):
                        r_copy(kind, half, phase, direction, piece, 1).wait_send()


def on_device(
    span_q, decode_q, k_cache, v_cache, span_k, span_v, decode_k, decode_v, decode_pos,
    out_weight, span_resid, decode_resid, norm_gain, router, span_expert, decode_expert,
    w_gate, w_up, w_down,
):
    tok, width = span_q.shape
    pre = k_cache.shape[0]
    model = out_weight.shape[1]
    hidden = w_gate.shape[2]
    quarter = model // 4
    piece_w = model // 8
    rows = tok // N_EXP
    vmem = pl.BlockSpec(memory_space=pltpu.VMEM)
    hbm = pl.BlockSpec(memory_space=pl.ANY)
    out = jax.ShapeDtypeStruct((rows, model), BF16)
    unit = (2, 16, piece_w)
    sems = [12, 60, 60, 24, 24, 24, 24, 6, 6, 6, 6, 8, 8, 24, 24, 16, 16, 120, 120, 48, 48, 16, 16]
    return pl.pallas_call(
        layer_kernel,
        out_shape=(out, out),
        in_specs=[vmem] * 13 + [hbm] * 6,
        out_specs=(vmem, vmem),
        scratch_shapes=[
            pltpu.VMEM((2, NY, NZ, 2, tok // 2, width), BF16),
            pltpu.VMEM((pre + HEAD, HEAD), BF16),
            pltpu.VMEM((pre + HEAD, 2 * HEAD), BF16),
            pltpu.VMEM((N_CTX, tok, HEAD), jnp.int32),
            pltpu.VMEM((2, 4, 4, tok, width), BF16),
            pltpu.VMEM((2, 4, 4, 16, HEAD), F32),
            pltpu.VMEM((2, 4, 3, tok, width), BF16),
            pltpu.VMEM((2, 4, 3, 16, HEAD), F32),
            pltpu.VMEM((2, 3, tok, width), BF16),
            pltpu.VMEM((2, 3, 16, HEAD), F32),
            pltpu.VMEM((2, 3, tok, width), BF16),
            pltpu.VMEM((2, 3, 16, HEAD), F32),
            pltpu.VMEM((2, tok, width), BF16),
            pltpu.VMEM((4, width, quarter), BF16),
            pltpu.VMEM((model, hidden), BF16),
            pltpu.VMEM((model, hidden), BF16),
            pltpu.VMEM((4, hidden, quarter), BF16),
            pltpu.VMEM((2, 4, N_X, 2 * rows, piece_w), BF16),
            pltpu.VMEM((2, 4, N_X, 2 * rows, piece_w), BF16),
            pltpu.VMEM((2, 4, N_X, 2 * rows, piece_w), BF16),
            pltpu.VMEM((2, 4, N_X - 1, 2 * rows, piece_w), BF16),
            pltpu.VMEM((2, rows, model), F32),
            pltpu.VMEM((2, 8 * rows, 16 * N_EXP), BF16),
            pltpu.VMEM((2, N_EXP, 16, piece_w), BF16),
            pltpu.VMEM((2, N_EXP, 16, piece_w), BF16),
            pltpu.VMEM((2, 4, NY, NZ) + unit, BF16),
            pltpu.VMEM((2, 4, NY, NZ) + unit, BF16),
            pltpu.VMEM((2, 2, 2, 4) + unit, BF16),
            pltpu.VMEM((2, 2, 2, 2, 4) + unit, BF16),
            pltpu.VMEM((2, 4, 4) + unit, BF16),
            pltpu.VMEM((2, 2, 2) + unit, BF16),
            pltpu.VMEM((2, 2, 2, 2) + unit, BF16),
            pltpu.VMEM((2, 4) + unit, BF16),
            pltpu.VMEM((2, N_EXP, 16, piece_w), BF16),
            pltpu.VMEM((2, N_EXP, 16, piece_w), BF16),
        ]
        + [pltpu.SemaphoreType.DMA((n,)) for n in sems],
        compiler_params=pltpu.CompilerParams(
            collective_id=0, has_side_effects=True, vmem_limit_bytes=62 * 2**20
        ),
        name="layer",
    )(
        span_q, decode_q, decode_pos.reshape(-1, HEAD), span_k, span_v, decode_k, decode_v,
        span_resid, decode_resid, norm_gain.reshape(1, model), router.T,
        span_expert.reshape(1, rows), decode_expert.reshape(1, rows),
        k_cache, v_cache, out_weight, w_gate, w_up, w_down,
    )


def solution(mesh):
    rows = P(("ctx", "exp"), None)
    both = P("ctx", "exp")
    in_specs = (
        (both,) * 8
        + (P(), P("exp", None), rows, rows, P(), P(), rows, rows)
        + (P("exp", None, "ctx"), P("exp", None, "ctx"), P("exp", "ctx", None))
    )
    return jax.shard_map(
        on_device, mesh=mesh, in_specs=in_specs, out_specs=(rows, rows), check_vma=False
    )
```

time: 740 us -> 180 us (0.24)
  waiting for transfers between devices: 359 us -> 0 us
  Pallas kernels: 0 us -> 175 us
  matrix products: 145 us -> 0 us
  blocking collectives: 84.9 us -> 0 us
  other arithmetic: 77.5 us -> 0 us
  local copies, waits for them, and re-layouts: 48.7 us -> 4.38 us
  between operations: 14.5 us -> 0.64 us
  loops' own time: 8.13 us -> 0 us
    reduce_scatter x3 -> x0, waiting for transfers between devices: 190 us -> none  [the longest x1 80.5 us: on_device(): lax.psum_scatter(scaled_numer, 'ctx', scatter_dimension=0, tiled=True)]
    pallas_call x0 -> x1, Pallas kernels: none -> 175 us  [on_device(): pl.pallas_call(layer_kernel, out_shape=(out, out), in_specs=[vmem] * 13 +...]
    dot_general x23 -> x0, matrix products: 145 us -> none  [the longest x4 57.6 us: attend_block(): jnp.einsum('bskgd,jkd->bskgj', queries, key_pre, preferred_element_type=j...]
    all_gather x2 -> x0, waiting for transfers between devices: 104 us -> none  [the longest x1 56.1 us: on_device(): shard_rows = lax.all_gather(arrived, 'ctx', axis=0, tiled=True)]
    unnamed x7 -> x0, waiting for transfers between devices: 64.3 us -> none
    reduce_sum x11 -> x0, other arithmetic: 62.6 us -> none  [the longest x8 61.1 us: attend_block(): denom_part = jnp.sum(weight_pre, -1) + jnp.sum(weight_span, -1)]
    pmax x1 -> x0, blocking collectives: 58.2 us -> none  [on_device(): top_every = lax.pmax(top_max, 'ctx')]
    all_to_all x2 -> x0, blocking collectives: 26.7 us -> none  [the longest x1 13.4 us: on_device(): lax.all_to_all(buffer, 'exp', split_axis=0, concat_axis=0, tiled=True)]
  transfers between devices with their start and end apart: 6 -> 0, of which waited for: 6 -> 0; matrix products, arithmetic and copies ran while one was open for 3% -> 0% of each run, Pallas kernels for 0% -> 0%
where the time goes in v2:
time: 180 us
  Pallas kernels  175 us (97%)
  local copies, waits for them, and re-layouts  4.38 us (2%)
    pallas_call x1, Pallas kernels, on_device(): pl.pallas_call(layer_kernel, out_shape=(out, out), in_specs=[vmem] * 13 +...  175 us

profile of v2, /device:TPU:1, one launch (start us, length us, event | category | flops | bytes accessed | tf_op | source)
XLA Modules:
  0.0 180.0 jit_solution(15776024609988991836)
XLA Ops:
  0.6 1.3 reshape.17.gain_ref
  2.0 175.0 %layer.1 = (bf16[8,5120]{1,0:T(8,128)(2,1)}, bf16[8,5120]{1,0:T(8,128)(2,1)}) custom-call(bf16[64,640]{1,0:T(8,128)(2,1)} %sq_ref.1, bf16[64,640]{1,0:T(8,128)(2,1)} %dq_ref.1, s32[8,128]{1,0:T(8,128)} %bitcast.5, bf16[64,128]{1,0:T(8,128)(2,1)} %sk_ref.1, bf16[64,128]{1,0:T(8,128)(2,1)} %sv_ref.1, bf16[64,128]{1,0:T(8,128)(2,1)} %dk_ref.1, ...), custom_call_target="tpu_custom_call" | custom-call | tf_op jit(solution)/shard_map/layer/pallas_call | solution.py:715
  177.0 1.5 copy.23
  178.5 1.5 copy.24

commit v3 on v2

--- a/solution.py
+++ b/solution.py
@@ -33,60 +33,64 @@
     )
 
 
-class Ring:
+class Gather:
     def __init__(self, ref, first, here, along, send, recv, base):
         self.ref, self.first, self.here, self.along = ref, first, here, along
         self.send, self.recv, self.base = send, recv, base
 
-    def copy(self, phase, line, direction, piece, hop):
-        axis = self.first if phase == 0 else 1 - self.first
+    def near_copy(self, step):
+        block = self.ref(None, *self.here)
+        index = self.base + step - 1
+        to = self.along(self.first, step)
+        return copy_to(block, block, self.send.at[index], self.recv.at[index], ctx=to)
+
+    def copy(self, line, direction, hop):
+        axis = 1 - self.first
         at = list(self.here)
         at[self.first] = (at[self.first] + line) % 4
-        step = 0 if hop == 0 else (3 if direction == 0 else 1)
-        at[axis] = (at[axis] + step) % 4
-        index = self.base + (0 if phase == 0 else 1 + line) * 6
-        index = index + (direction * 2 + piece if hop == 0 else 4 + direction)
-        block = self.ref(piece, at[0], at[1])
+        if hop == 1:
+            at[axis] = (at[axis] + (3 if direction == 0 else 1)) % 4
+        index = self.base + 3 + line * 4 + hop * 2 + direction
+        block = self.ref(None if hop == 0 else direction, at[0], at[1])
         to = self.along(axis, 1 if direction == 0 else 3)
         return copy_to(block, block, self.send.at[index], self.recv.at[index], ctx=to)
 
-    def start(self, phase, line):
-        for piece in range(2):
-            self.copy(phase, line, 0, piece, 0).start()
-            self.copy(phase, line, 1, 1 - piece, 0).start()
-
-    def forward(self, phase, line):
+    def begin(self):
+        for step in (1, 3, 2):
+            self.near_copy(step).start()
+
+    def arrived(self, step):
+        self.near_copy(step).wait_recv()
+
+    def start(self, line):
         for direction in range(2):
-            self.copy(phase, line, direction, direction, 0).wait_recv()
-            self.copy(phase, line, direction, direction, 1).start()
-
-    def near(self, phase, line):
+            self.copy(line, direction, 0).start()
+
+    def forward(self, line):
         for direction in range(2):
-            self.copy(phase, line, direction, 1 - direction, 0).wait_recv()
-
-    def far(self, phase, line):
+            self.copy(line, direction, 0).wait_recv()
+            self.copy(line, direction, 1).start()
+
+    def far(self, line):
         for direction in range(2):
-            self.copy(phase, line, direction, direction, 1).wait_recv()
-
-    def sent(self, phase, line):
-        for direction in range(2):
-            for piece in range(2):
-                self.copy(phase, line, direction, piece, 0).wait_send()
-            self.copy(phase, line, direction, direction, 1).wait_send()
+            self.copy(line, direction, 1).wait_recv()
 
     def all_sent(self):
-        self.sent(0, 0)
+        for step in range(1, 4):
+            self.near_copy(step).wait_send()
         for line in range(4):
-            self.sent(1, line)
+            for direction in range(2):
+                for hop in range(2):
+                    self.copy(line, direction, hop).wait_send()
 
 
 def layer_kernel(
-    sq_ref, dq_ref, pos_ref, sk_ref, sv_ref, dk_ref, dv_ref, sr_ref, dr_ref, gain_ref,
-    router_ref, se_ref, de_ref, k_hbm, v_hbm, ow_hbm, wg_hbm, wu_hbm, wd_hbm,
-    span_ref, dec_ref,
-    qb, kx, vx, pos_cols, num_out, stat_out, num_in, stat_in, mid_out, mid_stat, last_in,
+    sq_hbm, dq_hbm, k_hbm, v_hbm, sk_hbm, sv_hbm, ow_hbm, wg_hbm, wu_hbm, wd_hbm,
+    pos_hbm, dk_hbm, dv_hbm, sr_hbm, dr_hbm, gain_hbm, router_hbm, se_hbm, de_hbm,
+    out_ref,
+    pos_ref, dk_ref, dv_ref, sr_ref, dr_ref, gain_ref, router_ref, se_ref, de_ref, qb, kx, vx, pos_cols, num_out, stat_out, num_in, stat_in, mid_out, mid_stat, last_in,
     last_stat, attn, ow, wg, wu, wd, cout, cin, xout, xin, stream_ref, pick_ref, mout, min_,
-    xg, po, r1, r2, ph, r3, r4, fin, rout, rin,
+    xg, po, r1, r2, ph, r4, fin, rout, rin,
     w_sem, q_send, q_recv, n_send, n_recv, s_send, s_recv, l_send, l_recv, t_send, t_recv,
     c_send, c_recv, x_send, x_recv, a_send, a_recv, g_send, g_recv, r_send, r_recv,
     b_send, b_recv,
@@ -95,8 +99,8 @@
     here = (me_c // NZ, me_c % NZ)
     my_y, my_z = here
     my_x, my_k = me_e // 2, me_e % 2
-    tok = sq_ref.shape[0]
-    heads = sq_ref.shape[1] // HEAD
+    tok = sq_hbm.shape[0]
+    heads = sq_hbm.shape[1] // HEAD
     pre = k_hbm.shape[0]
     piece_w = xg.shape[-1]
     rows = tok // N_EXP
@@ -123,33 +127,35 @@
     quarter = 2 * piece_w
     loads = [load(0, k_hbm, kx.at[pl.ds(0, pre)])]
     loads += [load(1, v_hbm, vx.at[pl.ds(0, pre), pl.ds(0, HEAD)])]
+    early = [load(12, sq_hbm, qb.at[0, my_y, my_z]), load(13, dq_hbm, qb.at[1, my_y, my_z])]
+    early += [load(14, sk_hbm, kx.at[pl.ds(pre, tok)])]
+    early += [load(15, sv_hbm, vx.at[pl.ds(pre, tok), pl.ds(0, HEAD)])]
+    early += [load(16, pos_hbm, pos_ref)]
+    late = [
+        load(17 + i, src, dst)
+        for i, (src, dst) in enumerate(
+            [
+                (dk_hbm, dk_ref), (dv_hbm, dv_ref), (sr_hbm, sr_ref), (dr_hbm, dr_ref),
+                (gain_hbm, gain_ref), (router_hbm, router_ref), (se_hbm, se_ref),
+                (de_hbm, de_ref),
+            ]
+        )
+    ]
     loads += [load(2 + q, ow_hbm.at[:, pl.ds(q * quarter, quarter)], ow.at[q]) for q in range(4)]
     loads += [load(6, wg_hbm.at[0], wg), load(7, wu_hbm.at[0], wu)]
     loads += [load(8 + q, wd_hbm.at[0, :, pl.ds(q * quarter, quarter)], wd.at[q]) for q in range(4)]
-    for c in loads:
+    for c in early + loads[:2] + late:
         c.start()
 
-    for kind, ref in enumerate((sq_ref, dq_ref)):
-        for piece in range(2):
-            half = tok // 2
-            qb[kind, my_y, my_z, piece] = ref[piece * half : (piece + 1) * half]
-    q_rings = [
-        Ring(
-            lambda piece, y, z, kind=kind: qb.at[kind, y, z, piece],
-            1 - kind, here, along, q_send, q_recv, 30 * kind,
-        )
-        for kind in range(2)
-    ]
-    pl.semaphore_wait(barrier, N_EXP - 1 + 6)
-    q_rings[0].start(0, 0)
-    q_rings[0].start(1, 0)
+    def load_weights(first, last):
+        for c in loads[first:last]:
+            c.start()
 
     extra = kx.shape[0] - pre - tok
-    kx[pre : pre + tok] = sk_ref[...]
     kx[pre + tok :] = jnp.zeros((extra, HEAD), BF16)
-    vx[pre : pre + tok, :HEAD] = sv_ref[...]
     vx[pre + tok :, :HEAD] = jnp.zeros((extra, HEAD), BF16)
     vx[:, HEAD:] = jnp.ones((vx.shape[0], HEAD), BF16)
+    early[4].wait()
     pos_f = pos_ref[...].astype(F32)
     pos_f = jnp.concatenate(
         [pos_f, jnp.zeros((HEAD - pos_f.shape[0], HEAD), F32)], 0
@@ -160,18 +166,44 @@
         pos_cols[b] = jnp.broadcast_to(
             pos_f[start : start + tok, column : column + 1], (tok, HEAD)
         )
-    loads[0].wait()
-    loads[1].wait()
-
-    lane = lax.broadcasted_iota(jnp.int32, (tok, HEAD), 1)
-
-    def order(k):
-        later = (k + 1) % N_CTX
-        group, j = later // 4, later % 4
-        j = (j + 3 * ((4 - group) // 4)) % 4
+
+    def order(kind, k):
+        group, j = (k // 4 + kind) % 4, (k + kind) % 4
         line = (3 * group + 3 * (group * (group - 1) // 2)) % 4
         step = (3 * j + 3 * (j * (j - 1) // 2)) % 4
         return line, step
+
+    def query(kind, line, step):
+        if line is None:
+            block, index, to = qb.at[kind, my_y, my_z], kind * 15 + step - 1, along(1, step)
+        else:
+            block, index = qb.at[kind, my_y, (my_z + line) % NZ], kind * 15 + 2 + line * 3 + step
+            to = along(0, step)
+        return copy_to(block, block, q_send.at[index], q_recv.at[index], ctx=to)
+
+    def queries_z(kind):
+        for step in (1, 3, 2):
+            query(kind, None, step).start()
+
+    def queries_here(kind):
+        for step in (1, 3, 2):
+            query(kind, None, step).wait_recv()
+
+    def queries_y(kind, lines, steps):
+        for step in steps:
+            for line in lines:
+                query(kind, line, step).start()
+
+    early[0].wait()
+    early[1].wait()
+    pl.semaphore_wait(barrier, N_EXP - 1 + 6)
+
+    queries_z(0)
+    queries_y(0, (0,), (1,))
+    for c in early[2:4] + loads[:2] + late:
+        c.wait()
+
+    lane = lax.broadcasted_iota(jnp.int32, (tok, HEAD), 1)
 
     def n_copy(kind, line, step):
         index = kind * 12 + line * 3 + step - 1
@@ -217,7 +249,13 @@
         return top, out
 
     def attend(kind, k):
-        line, step = order(k)
+        line, step = order(kind, k)
+        across, z_line = (line, step) if kind == 0 else (step, line)
+
+        @pl.when(across != 0)
+        def _():
+            query(kind, z_line, (4 - across) % 4).wait_recv()
+
         shift = (line, step) if kind == 0 else (step, line)
         src_y, src_z = (my_y + shift[0]) % NY, (my_z + shift[1]) % NZ
         src = src_y * NZ + src_z
@@ -226,7 +264,7 @@
             limit = jnp.clip(src * tok + row - me_c * tok + 1, 0, tok)
         else:
             limit = pos_cols[src][:, :1] - me_c * pre
-        q = jnp.concatenate([qb[kind, src_y, src_z, 0], qb[kind, src_y, src_z, 1]], 0)
+        q = qb[kind, src_y, src_z]
         q = jnp.concatenate([q[:, h * HEAD : (h + 1) * HEAD] for h in range(heads)], 0)
         limit = jnp.concatenate([limit] * heads, 0)
 
@@ -314,7 +352,7 @@
             value = dv_ref[...].astype(F32)
             stat = jnp.full((tok, HEAD), NEG, F32)
             for h in range(heads):
-                query = dq_ref[:, h * HEAD : (h + 1) * HEAD].astype(F32)
+                query = qb[1, my_y, my_z, :, h * HEAD : (h + 1) * HEAD].astype(F32)
                 stat = jnp.where(lane == h, jnp.sum(query * key, -1, keepdims=True), stat)
             stat = jnp.concatenate([stat, jnp.full((HEAD - tok, HEAD), NEG, F32)], 0)
             top = stat.T[:8]
@@ -396,7 +434,7 @@
         normed = []
         for i, part in enumerate(pieces):
             columns = slice(i * piece_w, (i + 1) * piece_w)
-            part = (part * inverse * gain_ref[:, columns].astype(F32)).astype(BF16)
+            part = (part * inverse * gain_ref[columns].astype(F32).reshape(1, piece_w)).astype(BF16)
             normed.append(part)
             logits = logits + lax.dot_general(
                 part, router_ref[:, columns], (((1,), (1,)), ((), ())),
@@ -434,11 +472,19 @@
         wanted = (to_row % 16) // 2 * 16 + (to_row // 16) * 2 + to_row % 2
         return jnp.where(wanted == from_row, 1.0, 0.0).astype(BF16)
 
+    def x_block(kind, half):
+        def block(piece, y, z):
+            if piece is None:
+                return xg.at[kind, pl.ds(2 * half, 2), y, z]
+            return xg.at[kind, 2 * half + piece, y, z]
+
+        return block
+
     g_rings = [
         [
-            Ring(
-                lambda piece, y, z, kind=kind, half=half: xg.at[kind, 2 * half + piece, y, z],
-                1 - half, here, along, g_send, g_recv, (kind * 2 + half) * 30,
+            Gather(
+                x_block(kind, half), 1 - half, here, along, g_send, g_recv,
+                (kind * 2 + half) * 19,
             )
             for half in range(2)
         ]
@@ -453,99 +499,82 @@
         for i in range(8):
             xg[kind, i // 2, my_y, my_z, i % 2] = arrived[i * 16 : (i + 1) * 16]
         for ring in g_rings[kind]:
-            ring.start(0, 0)
+            ring.begin()
         for ring in g_rings[kind]:
-            ring.start(1, 0)
+            ring.start(0)
 
     def gather_b(kind):
-        for ring in g_rings[kind]:
-            ring.forward(0, 0)
-        for ring in g_rings[kind]:
-            ring.near(0, 0)
-            ring.start(1, 1)
-            ring.start(1, 3)
-
-    def gather_c(kind):
-        for ring in g_rings[kind]:
-            ring.forward(1, 0)
-        for ring in g_rings[kind]:
-            ring.far(0, 0)
-            ring.start(1, 2)
-
-    def gather_d(kind):
-        for line in (1, 3):
+        for step in (1, 3, 2):
             for ring in g_rings[kind]:
-                ring.forward(1, line)
-
-    def gather_e(kind):
-        for ring in g_rings[kind]:
-            ring.forward(1, 2)
+                ring.arrived(step)
+                ring.start((4 - step) % 4)
+
+    def gather_c(kind, *lines):
+        for line in lines:
+            for ring in g_rings[kind]:
+                ring.forward(line)
 
     def r_line(kind, q, axis, step):
         if axis == 0:
             return po.at[kind, q, (my_y + step) % NY]
         return po.at[kind, q, :, (my_z + step) % NZ]
 
-    def r_copy(kind, half, phase, direction, piece, hop):
-        axis = half if phase == 0 else 1 - half
+    def r_copy(kind, half, direction, piece, hop):
         q = 2 * half + piece
         step = 2 if hop == 0 else (1 if direction == 0 else 3)
-        index = (kind * 4 + half * 2 + phase) * 6
-        index = index + (4 + direction if hop == 0 else direction * 2 + piece)
-        if phase == 0:
-            src = r_line(kind, q, axis, step)
-            dst = r1.at[kind, half, direction] if hop == 0 else r2.at[kind, half, direction, piece]
-        else:
-            src = ph.at[kind, q, (here[axis] + step) % 4]
-            dst = r3.at[kind, half, direction] if hop == 0 else r4.at[kind, half, direction, piece]
+        index = (kind * 2 + half) * 9 + (4 + direction if hop == 0 else direction * 2 + piece)
+        dst = r1.at[kind, half, direction] if hop == 0 else r2.at[kind, half, direction, piece]
         return copy_to(
-            src, dst, r_send.at[index], r_recv.at[index],
-            ctx=along(axis, 1 if direction == 0 else 3),
-        )
-
-    def r_begin(kind, half, phase):
+            r_line(kind, q, half, step), dst, r_send.at[index], r_recv.at[index],
+            ctx=along(half, 1 if direction == 0 else 3),
+        )
+
+    def r_last(kind, half, step):
+        index = (kind * 2 + half) * 9 + 5 + step
+        axis = 1 - half
+        return copy_to(
+            ph.at[kind, half, (here[axis] + step) % 4], r4.at[kind, half, step - 1],
+            r_send.at[index], r_recv.at[index], ctx=along(axis, step),
+        )
+
+    def r_begin(kind, half):
         for direction in range(2):
-            r_copy(kind, half, phase, direction, direction, 0).start()
+            r_copy(kind, half, direction, direction, 0).start()
         for direction in range(2):
-            r_copy(kind, half, phase, direction, 1 - direction, 1).start()
-
-    def r_middle(kind, half, phase):
-        axis = half if phase == 0 else 1 - half
+            r_copy(kind, half, direction, 1 - direction, 1).start()
+
+    def r_middle(kind, half):
         for direction in range(2):
-            r_copy(kind, half, phase, direction, direction, 0).wait_recv()
+            r_copy(kind, half, direction, direction, 0).wait_recv()
             q = 2 * half + direction
-            step = 1 if direction == 0 else 3
-            if phase == 0:
-                line, arrived = r_line(kind, q, axis, step), r1.at[kind, half, direction]
-            else:
-                line, arrived = ph.at[kind, q, (here[axis] + step) % 4], r3.at[kind, half, direction]
-            line[...] = (line[...].astype(F32) + arrived[...].astype(F32)).astype(BF16)
-            r_copy(kind, half, phase, direction, direction, 1).start()
-
-    def r_finish(kind, half, phase):
-        axis = half if phase == 0 else 1 - half
+            line = r_line(kind, q, half, 1 if direction == 0 else 3)
+            arrived = r1[kind, half, direction].astype(F32)
+            line[...] = (line[...].astype(F32) + arrived).astype(BF16)
+            r_copy(kind, half, direction, direction, 1).start()
+
+    def r_middle_done(kind, half):
         for direction in range(2):
             for piece in range(2):
-                r_copy(kind, half, phase, direction, piece, 1).wait_recv()
+                r_copy(kind, half, direction, piece, 1).wait_recv()
         for piece in range(2):
-            q = 2 * half + piece
-            if phase == 0:
-                own, arrived = r_line(kind, q, axis, 0), r2
-            else:
-                own, arrived = ph.at[kind, q, here[axis]], r4
-            total = own[...].astype(F32)
+            total = r_line(kind, 2 * half + piece, half, 0)[...].astype(F32)
             for direction in range(2):
-                total = total + arrived[kind, half, direction, piece].astype(F32)
-            if phase == 0:
-                ph[kind, q] = total.astype(BF16)
-            else:
-                fin[kind, q] = total.astype(BF16)
+                total = total + r2[kind, half, direction, piece].astype(F32)
+            ph[kind, half, :, piece] = total.astype(BF16)
+        for step in (2, 1, 3):
+            r_last(kind, half, step).start()
+
+    def r_finish(kind, half):
+        total = ph[kind, half, here[1 - half]].astype(F32)
+        for step in (1, 3, 2):
+            r_last(kind, half, step).wait_recv()
+            total = total + r4[kind, half, step - 1].astype(F32)
+        fin[kind, pl.ds(2 * half, 2)] = total.astype(BF16)
 
     def experts(kind):
         for line in range(4):
             for ring in g_rings[kind]:
-                ring.near(1, line)
-                ring.far(1, line)
+                ring.far(line)
         if kind == 0:
             loads[6].wait()
             loads[7].wait()
@@ -569,24 +598,19 @@
                     NY, NZ, 16, piece_w
                 )
             if q % 2 == 1:
-                r_begin(kind, q // 2, 0)
+                r_begin(kind, q // 2)
 
     def sums_b(kind):
         for half in range(2):
-            r_middle(kind, half, 0)
+            r_middle(kind, half)
 
     def sums_c(kind):
         for half in range(2):
-            r_finish(kind, half, 0)
-            r_begin(kind, half, 1)
-
-    def sums_d(kind):
-        for half in range(2):
-            r_middle(kind, half, 1)
+            r_middle_done(kind, half)
 
     def give_back(kind):
         for half in range(2):
-            r_finish(kind, half, 1)
+            r_finish(kind, half)
         back = jnp.dot(
             swap(), fin[kind].reshape(16 * N_EXP, piece_w), preferred_element_type=F32
         ).astype(BF16)
@@ -599,59 +623,49 @@
     def write(kind):
         for k in range(1, N_EXP):
             b_copy(kind, k).wait_recv()
-        out_ref = span_ref if kind == 0 else dec_ref
         result = jnp.dot(
             pick_ref[kind], rin[kind].reshape(16 * N_EXP, piece_w), preferred_element_type=F32
         )
         for i in range(8):
             columns = slice(i * piece_w, (i + 1) * piece_w)
             part = stream_ref[kind, :, columns] + result[i * rows : (i + 1) * rows]
-            out_ref[:, columns] = part.astype(BF16)
-
-    qs, qd = q_rings
+            out_ref[kind, :, columns] = part.astype(BF16)
 
     def do(f, *args):
         return lambda: f(*args)
 
     span_steps = {
-        0: [do(qs.forward, 0, 0), do(qs.near, 0, 0), do(qs.start, 1, 1), do(qs.start, 1, 3),
-            do(qd.start, 0, 0), do(qd.start, 1, 0)],
-        1: [do(qs.forward, 1, 0), do(qs.far, 0, 0), do(qs.start, 1, 2), do(qs.forward, 1, 3)],
-        2: [do(qs.forward, 1, 1), do(qs.near, 1, 0), do(qd.forward, 0, 0), do(qd.near, 0, 0),
-            do(qd.start, 1, 1), do(qd.start, 1, 3)],
-        3: [do(qs.forward, 1, 2), do(qs.near, 1, 3), do(qd.forward, 1, 0), do(qd.far, 0, 0),
-            do(qd.start, 1, 2)],
-        4: [do(qs.near, 1, 1), do(qd.forward, 1, 3), do(qd.forward, 1, 1)],
-        5: [do(qs.near, 1, 2), do(qd.forward, 1, 2)],
-        8: [do(merge_line, 0, 3), do(qd.near, 1, 0)],
-        9: [do(qd.near, 1, 3)],
-        10: [do(qs.far, 1, 0), do(qs.far, 1, 3), do(qd.near, 1, 1)],
-        11: [do(qs.far, 1, 1), do(qs.far, 1, 2), do(qd.near, 1, 2)],
-        12: [do(merge_line, 0, 1)],
-        13: [do(qd.far, 1, 0), do(qd.far, 1, 3)],
-        14: [do(qd.far, 1, 1), do(qd.far, 1, 2)],
+        0: [do(queries_here, 0), do(queries_y, 0, (3, 1, 2), (1,))],
+        2: [do(queries_y, 0, (0, 3, 1, 2), (3,))],
+        4: [do(load_weights, 2, 6)],
+        5: [do(queries_y, 0, (0, 3, 1, 2), (2,))],
+        6: [do(queries_z, 1)],
+        8: [do(load_weights, 6, 8)],
+        9: [do(queries_here, 1), do(queries_y, 1, (3, 1), (1, 3, 2))],
+        10: [do(merge_line, 0, 3)],
+        12: [do(load_weights, 8, 12)],
+        13: [do(queries_y, 1, (2, 0), (1, 3, 2))],
+        14: [do(merge_line, 0, 1)],
     }
     dec_steps = {
-        0: [do(merge_line, 0, 2)],
-        2: [do(merge_rows, 0), do(project, 0)],
-        4: [do(chip_sum, 0)],
-        7: [do(route, 0)],
-        8: [do(merge_line, 1, 3)],
-        9: [do(gather_a, 0)],
-        10: [do(gather_b, 0)],
-        11: [do(gather_c, 0)],
-        12: [do(merge_line, 1, 1), do(gather_d, 0)],
-        13: [do(gather_e, 0)],
+        1: [do(merge_line, 0, 2)],
+        3: [do(merge_rows, 0), do(project, 0)],
+        5: [do(chip_sum, 0), do(merge_line, 1, 3)],
+        8: [do(route, 0)],
+        9: [do(merge_line, 1, 1)],
+        11: [do(gather_a, 0)],
+        13: [do(merge_line, 1, 2)],
+        14: [do(gather_b, 0)],
     }
     tail = [
-        do(merge_line, 1, 2), do(experts, 0), do(merge_rows, 1), do(project, 1), do(sums_b, 0),
-        do(chip_sum, 1), do(sums_c, 0), do(route, 1), do(sums_d, 0), do(gather_a, 1),
-        do(give_back, 0), do(gather_b, 1), do(gather_c, 1), do(gather_d, 1), do(write, 0),
-        do(gather_e, 1), do(experts, 1), do(sums_b, 1), do(sums_c, 1), do(sums_d, 1),
-        do(give_back, 1), do(write, 1),
+        do(merge_rows, 1), do(project, 1), do(chip_sum, 1), do(gather_c, 0, 0, 1, 3),
+        do(gather_c, 0, 2), do(route, 1), do(experts, 0), do(gather_a, 1), do(sums_b, 0),
+        do(gather_b, 1), do(sums_c, 0), do(gather_c, 1, 0, 1, 3), do(gather_c, 1, 2),
+        do(experts, 1), do(sums_b, 1), do(give_back, 0),
+        do(sums_c, 1), do(give_back, 1), do(write, 0), do(write, 1),
     ]
 
-    def loop(kind, steps):
+    def loop(kind, count, steps):
         def one(k, carry):
             attend(kind, k)
             for at, actions in steps.items():
@@ -663,15 +677,20 @@
 
             return carry
 
-        lax.fori_loop(0, N_CTX, one, 0)
-
-    loop(0, span_steps)
-    loop(1, dec_steps)
+        lax.fori_loop(0, count, one, 0)
+
+    attend(1, N_CTX - 1)
+    loop(0, N_CTX, span_steps)
+    loop(1, N_CTX - 1, dec_steps)
     for action in tail:
         action()
 
     for kind in range(2):
-        q_rings[kind].all_sent()
+        for step in range(1, 4):
+            query(kind, None, step).wait_send()
+            for line in range(4):
+                query(kind, line, step).wait_send()
+    for kind in range(2):
         for line in range(4):
             for step in range(1, 4):
                 for c in n_copy(kind, line, step):
@@ -688,11 +707,12 @@
             b_copy(kind, k).wait_send()
         for half in range(2):
             g_rings[kind][half].all_sent()
-            for phase in range(2):
-                for direction in range(2):
-                    r_copy(kind, half, phase, direction, direction, 0).wait_send()
-                    for piece in range(2):
-                        r_copy(kind, half, phase, direction, piece, 1).wait_send()
+            for direction in range(2):
+                r_copy(kind, half, direction, direction, 0).wait_send()
+                for piece in range(2):
+                    r_copy(kind, half, direction, piece, 1).wait_send()
+            for step in range(1, 4):
+                r_last(kind, half, step).wait_send()
 
 
 def on_device(
@@ -709,16 +729,25 @@
     rows = tok // N_EXP
     vmem = pl.BlockSpec(memory_space=pltpu.VMEM)
     hbm = pl.BlockSpec(memory_space=pl.ANY)
-    out = jax.ShapeDtypeStruct((rows, model), BF16)
+    out = jax.ShapeDtypeStruct((2, rows, model), BF16)
     unit = (2, 16, piece_w)
-    sems = [12, 60, 60, 24, 24, 24, 24, 6, 6, 6, 6, 8, 8, 24, 24, 16, 16, 120, 120, 48, 48, 16, 16]
-    return pl.pallas_call(
+    sems = [25, 31, 31, 24, 24, 24, 24, 6, 6, 6, 6, 8, 8, 24, 24, 16, 16, 76, 76, 36, 36, 16, 16]
+    both = pl.pallas_call(
         layer_kernel,
-        out_shape=(out, out),
-        in_specs=[vmem] * 13 + [hbm] * 6,
-        out_specs=(vmem, vmem),
+        out_shape=out,
+        in_specs=[hbm] * 19,
+        out_specs=vmem,
         scratch_shapes=[
-            pltpu.VMEM((2, NY, NZ, 2, tok // 2, width), BF16),
+            pltpu.VMEM((N_CTX * tok // HEAD, HEAD), jnp.int32),
+            pltpu.VMEM((tok, HEAD), BF16),
+            pltpu.VMEM((tok, HEAD), BF16),
+            pltpu.VMEM((rows, model), BF16),
+            pltpu.VMEM((rows, model), BF16),
+            pltpu.VMEM((model,), BF16),
+            pltpu.VMEM((N_EXP, model), BF16),
+            pltpu.VMEM((1, rows), jnp.int32),
+            pltpu.VMEM((1, rows), jnp.int32),
+            pltpu.VMEM((2, NY, NZ, tok, width), BF16),
             pltpu.VMEM((pre + HEAD, HEAD), BF16),
             pltpu.VMEM((pre + HEAD, 2 * HEAD), BF16),
             pltpu.VMEM((N_CTX, tok, HEAD), jnp.int32),
@@ -747,9 +776,8 @@
             pltpu.VMEM((2, 4, NY, NZ) + unit, BF16),
             pltpu.VMEM((2, 2, 2, 4) + unit, BF16),
             pltpu.VMEM((2, 2, 2, 2, 4) + unit, BF16),
-            pltpu.VMEM((2, 4, 4) + unit, BF16),
-            pltpu.VMEM((2, 2, 2) + unit, BF16),
-            pltpu.VMEM((2, 2, 2, 2) + unit, BF16),
+            pltpu.VMEM((2, 2, 4, 2) + unit, BF16),
+            pltpu.VMEM((2, 2, 3, 2) + unit, BF16),
             pltpu.VMEM((2, 4) + unit, BF16),
             pltpu.VMEM((2, N_EXP, 16, piece_w), BF16),
             pltpu.VMEM((2, N_EXP, 16, piece_w), BF16),
@@ -760,11 +788,12 @@
         ),
         name="layer",
     )(
-        span_q, decode_q, decode_pos.reshape(-1, HEAD), span_k, span_v, decode_k, decode_v,
-        span_resid, decode_resid, norm_gain.reshape(1, model), router.T,
-        span_expert.reshape(1, rows), decode_expert.reshape(1, rows),
-        k_cache, v_cache, out_weight, w_gate, w_up, w_down,
+        span_q, decode_q, k_cache, v_cache, span_k, span_v, out_weight, w_gate, w_up, w_down,
+        decode_pos.reshape(-1, HEAD), decode_k, decode_v, span_resid, decode_resid,
+        norm_gain, router.T, span_expert.reshape(1, rows),
+        decode_expert.reshape(1, rows),
     )
+    return both[0], both[1]
 
 
 def solution(mesh):

time: 180 us -> 168 us (0.933)
  Pallas kernels: 175 us -> 166 us
  local copies, waits for them, and re-layouts: 4.38 us -> 1.6 us
    pallas_call x1, Pallas kernels: 175 us -> 166 us  [on_device(): pl.pallas_call(layer_kernel, out_shape=out, in_specs=[hbm] * 19, out_spec...]
    unnamed x2 -> x0, local copies, waits for them, and re-layouts: 3.05 us -> none
where the time goes in v3:
time: 168 us
  Pallas kernels  166 us (99%)
    pallas_call x1, Pallas kernels, on_device(): pl.pallas_call(layer_kernel, out_shape=out, in_specs=[hbm] * 19, out_spec...  166 us

profile of v3, /device:TPU:1, one launch (start us, length us, event | category | flops | bytes accessed | tf_op | source)
XLA Modules:
  0.0 168.1 jit_solution(17017678376676755275)
XLA Ops:
  0.6 165.9 %layer.1 = bf16[2,8,5120]{2,1,0:T(8,128)(2,1)} custom-call(bf16[64,640]{1,0:T(8,128)(2,1)} %sq_hbm.1, bf16[64,640]{1,0:T(8,128)(2,1)} %dq_hbm.1, bf16[3072,128]{1,0:T(8,128)(2,1)} %k_hbm.1, bf16[3072,128]{1,0:T(8,128)(2,1)} %v_hbm.1, bf16[64,128]{1,0:T(8,128)(2,1)} %sk_hbm.1, bf16[64,128]{1,0:T(8,128)(2,1)} %sv_hbm.1, bf16[640,5120]{1,0:T(8,128)(2,1)} %ow_hbm.1, ...), custom_call_target="tpu_custom_call" | custom-call | tf_op jit(solution)/shard_map/layer/pallas_call | solution.py:735
  166.5 1.6 slice_bitcast_fusion

commit v4 on v3

--- a/solution.py
+++ b/solution.py
@@ -271,9 +271,12 @@
         def mask(s, lo):
             if kind == 0 and lo + s.shape[1] <= pre:
                 return s
+            if kind == 0:
+                cached, s = s[:, : pre - lo], s[:, pre - lo :]
+                column = lax.broadcasted_iota(jnp.int32, s.shape, 1)
+                return jnp.concatenate([cached, jnp.where(column < limit, s, NEG)], 1)
             column = lax.broadcasted_iota(jnp.int32, s.shape, 1)
-            hidden_from = limit + (pre - lo) if kind == 0 else limit - lo
-            return jnp.where(column < hidden_from, s, NEG)
+            return jnp.where(column < limit - lo, s, NEG)
 
         state = None
         last = kx.shape[0] if kind == 0 else pre

time: 168 us -> 168 us (level)
  no operation moved by 1% of the time
where the time goes in v4:
time: 168 us
  Pallas kernels  166 us (99%)
    pallas_call x1, Pallas kernels, on_device(): pl.pallas_call(layer_kernel, out_shape=out, in_specs=[hbm] * 19, out_spec...  166 us

profile of v4, /device:TPU:1, one launch (start us, length us, event | category | flops | bytes accessed | tf_op | source)
XLA Modules:
  0.0 168.1 jit_solution(8956582067760701906)
XLA Ops:
  0.6 165.8 %layer.1 = bf16[2,8,5120]{2,1,0:T(8,128)(2,1)} custom-call(bf16[64,640]{1,0:T(8,128)(2,1)} %sq_hbm.1, bf16[64,640]{1,0:T(8,128)(2,1)} %dq_hbm.1, bf16[3072,128]{1,0:T(8,128)(2,1)} %k_hbm.1, bf16[3072,128]{1,0:T(8,128)(2,1)} %v_hbm.1, bf16[64,128]{1,0:T(8,128)(2,1)} %sk_hbm.1, bf16[64,128]{1,0:T(8,128)(2,1)} %sv_hbm.1, bf16[640,5120]{1,0:T(8,128)(2,1)} %ow_hbm.1, ...), custom_call_target="tpu_custom_call" | custom-call | tf_op jit(solution)/shard_map/layer/pallas_call | solution.py:738
  166.5 1.6 slice_bitcast_fusion
